TPU v7x, 128 devices: a whole 4x4x4 slice. The times are simulated.
128 devices in a mesh: region: 8 (over y, core), tile: 16 (over z, x).
Axes of the slice: x: 4, y: 4, z: 4, core: 2. Of those that a mesh axis runs over, the one named last changes fastest.
Arguments:
- coeffs: float32 [4, 2048, 2048], P(None, 'tile', 'region')
- obs_cell: int32 [131072], P(('region', 'tile')), may hold values from 0 to 524287
- obs_value: float32 [8, 131072], P(None, ('region', 'tile')), may hold values from -6 to 6
- obs_count: int32 [128], P(('region', 'tile')), may hold values from 1 to 1024, 81920 in all
Outputs:
- solution_field: float32 [2048, 8, 2048], P('tile', None, 'region')
- residual: float32 [2048, 8, 2048], P('tile', None, 'region')
Inputs may be any that keep to these rules, and one draw needn't show every extreme that they name: `obs_cell`: cell number y * 256 + x within the owning region's 2048 x 256 cells. `obs_count`: live slots stand at the head of each device's block; some device has all 1024 live.
All inputs are finite; a program needn't handle non-finite values.
Results may differ from a plain program's by a relative error of at most 0.00029.
Values sent between devices are 32-bit elements; how exact they have to be, the bound alone decides.
No kernel may reach another device: no remote copies, remote signals or barrier semaphores. Data moves between devices by JAX's collectives and lax.ppermute only.
A program may use at most 128 MiB of HBM per device.

v0:
```python
import jax
import jax.numpy as jnp
from jax import lax
from jax.sharding import PartitionSpec as P

ITERS = 2


noise_var = 0.5
prec_scale = 0.01


def with_halo(x, sides, width):
    for axis, dim in sides:
        size, length = (lax.axis_size(axis), x.shape[dim])
        up = [(i, (i + 1) % size) for i in range(size - 1)]
        down = [(j, i) for i, j in up]
        last = lax.slice_in_dim(x, length - width, length, axis=dim)
        leading = lax.slice_in_dim(x, 0, width, axis=dim)
        before = lax.ppermute(last, axis, up)
        after = lax.ppermute(leading, axis, down)
        x = jnp.concatenate([before, x, after], axis=dim)
    return x


def stencil(padded, coef):
    along_x = coef[0]
    along_y = coef[1]
    mixed = coef[2]
    reaction = coef[3]
    centre = padded[1:-1, :, 1:-1]
    east_cell = padded[1:-1, :, 2:]
    west_cell = padded[1:-1, :, :-2]
    north_cell = padded[2:, :, 1:-1]
    south_cell = padded[:-2, :, 1:-1]
    north_east = padded[2:, :, 2:]
    north_west = padded[2:, :, :-2]
    south_east = padded[:-2, :, 2:]
    south_west = padded[:-2, :, :-2]
    middle_x = along_x[1:-1, 1:-1]
    middle_y = along_y[1:-1, 1:-1]
    east_face = (0.5 * (along_x[1:-1, 2:] + middle_x))[:, None, :]
    west_face = (0.5 * (along_x[1:-1, :-2] + middle_x))[:, None, :]
    north_face = (0.5 * (along_y[2:, 1:-1] + middle_y))[:, None, :]
    south_face = (0.5 * (along_y[:-2, 1:-1] + middle_y))[:, None, :]
    diffusion = east_face * (east_cell - centre) - west_face * (centre - west_cell)
    diffusion = diffusion + north_face * (north_cell - centre) - south_face * (centre - south_cell)
    cross_term = mixed[1:-1, 2:][:, None, :] * (north_east - south_east) - mixed[1:-1, :-2][
        :, None, :
    ] * (north_west - south_west)
    cross_term = (
        cross_term
        + mixed[2:, 1:-1][:, None, :] * (north_east - north_west)
        - mixed[:-2, 1:-1][:, None, :] * (south_east - south_west)
    )
    return reaction[1:-1, 1:-1][:, None, :] * centre - diffusion - 0.25 * cross_term


def local(coeffs, obs_cell, obs_value, obs_count):
    reals = obs_value.shape[0]
    rows_dev = coeffs.shape[1]
    cols_dev = coeffs.shape[2]
    slots_dev = obs_cell.shape[0]
    coef_pad = with_halo(coeffs, (("region", 2), ("tile", 1)), 2)
    inner_coef = coef_pad[:, 1:-1, 1:-1]
    live_slots = jnp.arange(slots_dev, dtype=jnp.int32) < obs_count[0]
    row_y = obs_cell // cols_dev
    col_x = obs_cell % cols_dev
    weight = jnp.where(live_slots, 1.0, 0.0).astype(jnp.float32)
    row_ids = jnp.arange(rows_dev * lax.axis_size("tile"), dtype=jnp.int32)
    row_hot = (
        jnp.where(row_y[:, None] == row_ids[None, :], 1.0, 0.0).astype(jnp.float32)
        * weight[:, None]
    )
    col_hot = jnp.where(
        col_x[:, None] == jnp.arange(cols_dev, dtype=jnp.int32)[None, :], 1.0, 0.0
    ).astype(jnp.float32)
    stacked = jnp.concatenate([obs_value, jnp.ones((1, obs_cell.shape[0]), jnp.float32)], axis=0)
    spread = (jnp.transpose(stacked)[:, :, None] * col_hot[:, None, :]).reshape(
        obs_cell.shape[0], (reals + 1) * cols_dev
    )
    term = jnp.dot(
        jnp.transpose(row_hot),
        spread,
        precision=lax.Precision.HIGHEST,
        preferred_element_type=jnp.float32,
    )
    summed = lax.psum_scatter(
        term.reshape(rows_dev * lax.axis_size("tile"), reals + 1, cols_dev),
        "tile",
        scatter_dimension=0,
        tiled=True,
    )
    right_side = summed[:, :reals, :] / noise_var
    obs_weight = summed[:, reals:, :] / noise_var

    def thin_rims(field):
        return with_halo(field, (("region", 2), ("tile", 0)), 1)

    def squares(current):
        return lax.psum(jnp.sum(current * current, axis=(0, 2)), ("region", "tile"))

    solution_field = jnp.zeros_like(right_side)
    residual = right_side
    direction = right_side
    norm_now = squares(residual)
    for iteration in range(ITERS):
        first = stencil(thin_rims(direction), inner_coef)
        second = stencil(thin_rims(first), inner_coef)
        image = prec_scale * second + obs_weight * direction
        alpha = norm_now / lax.psum(jnp.sum(direction * image, axis=(0, 2)), ("region", "tile"))
        solution_field = solution_field + alpha[None, :, None] * direction
        residual = residual - alpha[None, :, None] * image
        norm_next = squares(residual)
        direction = residual + (norm_next / norm_now)[None, :, None] * direction
        norm_now = norm_next
    return (solution_field, residual)


def solution(mesh):
    placed = (
        P(None, "tile", "region"),
        P(("region", "tile")),
        P(None, ("region", "tile")),
        P(("region", "tile")),
    )
    return jax.shard_map(
        local,
        mesh=mesh,
        in_specs=placed,
        out_specs=(P("tile", None, "region"), P("tile", None, "region")),
        check_vma=False,
    )
```

profile of v0, /device:TPU:1, one launch (start us, length us, event | category | flops | bytes accessed | tf_op | source)
XLA Modules:
  0.0 509.7 jit_solution(9215454465094936947)
XLA Ops:
  10.7 63.7 %fusion = f32[2048,9,256]{2,0,1:T(8,128)} fusion(f32[1024]{0:T(1024)S(1)} %fusion.67, s32[1024]{0:T(1024)S(1)} %get-tuple-element.57, f32[9,256,1024]{2,1,0:T(8,128)S(1)} %fusion.86), kind=kOutput, calls=%fused_computation | convolution fusion | flops 57988349952 | bytes 28319744 | tf_op jit(solution)/shard_map/dot_general | solution.py:82
  75.6 4.6 collective-permute-start
  80.2 1.9 collective-permute-start.1
  83.4 4.4 collective-permute-done.1
  87.9 3.1 collective-permute-start.2
  92.4 3.7 collective-permute-done.3
  96.8 102.3 %reduce-scatter.2.cloned.1.call-done = f32[128,9,256]{2,0,1:T(8,128)} async-done(((f32[2048,9,256]{2,0,1:T(8,128)}), f32[128,9,256]{2,0,1:T(8,128)}) %reduce-scatter.2.cloned.1.call-update) | async-done | bytes 1179664 | tf_op jit(solution)/shard_map/reduce_scatter | solution.py:88
  200.6 2.6 collective-permute-start.4
  203.2 3.2 collective-permute-start.5
  206.7 4.5 collective-permute-done.4
  213.8 4.0 collective-permute-start.7
  219.8 1.9 fusion.52
  221.9 1.9 collective-permute-start.8
  223.8 5.5 %collective-permute-start.9 = (f32[128,8,1]{2,0,1:T(8,128)S(1)}, f32[128,8,1]{2,0,1:T(8,128)S(1)}, u32[]{:S(2)}, u32[]{:S(2)}) collective-permute-start(f32[128,8,1]{2,0,1:T(8,128)S(1)} %get-tuple-element.35), channel_id=1, source_target_pairs={{0,16},{16,32},{32,48},{48,64},{64,80},{80,96},{96,112},{1,17},{17... | collective-permute-start | bytes 12296 | tf_op jit(solution)/shard_map/ppermute | solution.py:20
  229.3 4.9 collective-permute-done.8
  236.9 4.5 collective-permute-start.11
  243.5 2.3 multiply_reduce_fusion.2
  245.8 72.3 %all-reduce.1 = (f32[8]{0:T(128)S(1)}, f32[8]{0:T(128)S(1)}) all-reduce(f32[8]{0:T(128)S(1)} %get-tuple-element.5, f32[8]{0:T(128)S(1)} %get-tuple-element.4), channel_id=1, replica_groups=mesh['region'=8,'tile'=16] {'region','tile'}, use_global_device_ids=true, to_apply=%region_2.3 | all-reduce | flops 16 | bytes 128 | tf_op jit(solution)/shard_map/psum | solution.py:101
  318.5 62.5 %psum.30 = f32[8]{0:T(128)S(1)} all-reduce(f32[8]{0:T(128)S(1)} %get-tuple-element.12), channel_id=1, replica_groups=mesh['region'=8,'tile'=16] {'region','tile'}, use_global_device_ids=true, to_apply=%region_6.7 | all-reduce | flops 8 | bytes 64 | tf_op jit(solution)/shard_map/psum | solution.py:101
  381.4 2.5 collective-permute-start.12
  383.9 3.1 collective-permute-start.13
  387.0 4.9 collective-permute-done.12
  394.6 4.3 collective-permute-start.15
  400.8 1.9 fusion.28
  402.9 1.9 collective-permute-start.16
  404.8 5.5 %collective-permute-start.17 = (f32[128,8,1]{2,0,1:T(8,128)S(1)}, f32[128,8,1]{2,0,1:T(8,128)S(1)}, u32[]{:S(2)}, u32[]{:S(2)}) collective-permute-start(f32[128,8,1]{2,0,1:T(8,128)S(1)} %get-tuple-element.31), channel_id=1, source_target_pairs={{0,16},{16,32},{32,48},{48,64},{64,80},{80,96},{96,112},{1,17},{17... | collective-permute-start | bytes 12296 | tf_op jit(solution)/shard_map/ppermute | solution.py:20
  410.4 4.9 collective-permute-done.16
  417.9 4.5 collective-permute-start.19
  424.5 3.1 multiply_reduce_fusion
  427.6 70.5 %psum.31 = f32[8]{0:T(128)S(1)} all-reduce(f32[8]{0:T(128)S(1)} %get-tuple-element.10), channel_id=1, replica_groups=mesh['region'=8,'tile'=16] {'region','tile'}, use_global_device_ids=true, to_apply=%region_8.9 | all-reduce | flops 8 | bytes 64 | tf_op jit(solution)/shard_map/psum | solution.py:111
  499.7 1.6 copy.6
  501.2 1.6 copy.7
  (85 shorter events, 30.1 us)
Async XLA Ops:
  7.2 191.9 %reduce-scatter.2.cloned.1.call-start = ((), (), s32[]{:S(2)}) async-start(), calls=%async_computation.1 | async-start | bytes 20054016 | tf_op jit(solution)/shard_map/reduce_scatter | solution.py:88
  75.6 7.9 %collective-permute-start = (f32[4,128,2]{2,1,0:T(8,128)S(1)}, f32[4,128,2]{2,1,0:T(8,128)S(1)}, u32[]{:S(2)}, u32[]{:S(2)}) collective-permute-start(f32[4,128,2]{2,1,0:T(8,128)S(1)} %get-tuple-element.45), channel_id=1, source_target_pairs={{0,16},{16,32},{32,48},{48,64},{64,80},{80,96},{96,112},{1,17},{17... | collective-permute-start | bytes 12296 | tf_op jit(solution)/shard_map/ppermute | solution.py:20
  80.2 7.7 %collective-permute-start.1 = (f32[4,128,2]{2,1,0:T(8,128)S(1)}, f32[4,128,2]{2,1,0:T(8,128)S(1)}, u32[]{:S(2)}, u32[]{:S(2)}) collective-permute-start(f32[4,128,2]{2,1,0:T(8,128)S(1)} %get-tuple-element.46), channel_id=1, source_target_pairs={{16,0},{32,16},{48,32},{64,48},{80,64},{96,80},{112,96},{17,1},{33... | collective-permute-start | bytes 12296 | tf_op jit(solution)/shard_map/ppermute | solution.py:21
  87.9 4.4 collective-permute-start.2
  91.1 5.0 collective-permute-start.3
  200.6 10.6 %collective-permute-start.4 = (f32[128,8,1]{2,0,1:T(8,128)S(1)}, f32[128,8,1]{2,0,1:T(8,128)S(1)}, u32[]{:S(2)}, u32[]{:S(2)}) collective-permute-start(f32[128,8,1]{2,0,1:T(8,128)S(1)} %get-tuple-element.38), channel_id=1, source_target_pairs={{16,0},{32,16},{48,32},{64,48},{80,64},{96,80},{112,96},{17,1},{33... | collective-permute-start | bytes 12296 | tf_op jit(solution)/shard_map/ppermute | solution.py:21
  203.2 9.1 %collective-permute-start.5 = (f32[128,8,1]{2,0,1:T(8,128)S(1)}, f32[128,8,1]{2,0,1:T(8,128)S(1)}, u32[]{:S(2)}, u32[]{:S(2)}) collective-permute-start(f32[128,8,1]{2,0,1:T(8,128)S(1)} %get-tuple-element.37), channel_id=1, source_target_pairs={{0,16},{16,32},{32,48},{48,64},{64,80},{80,96},{96,112},{1,17},{17... | collective-permute-start | bytes 12296 | tf_op jit(solution)/shard_map/ppermute | solution.py:20
  206.6 36.8 %copy-start.6 = (f32[128,256]{1,0:T(8,128)}, f32[128,256]{1,0:T(8,128)S(1)}, u32[]{:S(2)}) copy-start(f32[128,256]{1,0:T(8,128)S(1)} %get-tuple-element.63) | copy-start | bytes 393220
  206.6 36.8 %copy-start.8 = (f32[128,256]{1,0:T(8,128)}, f32[128,256]{1,0:T(8,128)S(1)}, u32[]{:S(2)}) copy-start(f32[128,256]{1,0:T(8,128)S(1)} %get-tuple-element.64) | copy-start | bytes 393220
  206.7 36.8 %copy-start.10 = (f32[128,256]{1,0:T(8,128)}, f32[128,256]{1,0:T(8,128)S(1)}, u32[]{:S(2)}) copy-start(f32[128,256]{1,0:T(8,128)S(1)} %get-tuple-element.65) | copy-start | bytes 393220
  206.7 36.8 %copy-start.12 = (f32[128,256]{1,0:T(8,128)}, f32[128,256]{1,0:T(8,128)S(1)}, u32[]{:S(2)}) copy-start(f32[128,256]{1,0:T(8,128)S(1)} %get-tuple-element.66) | copy-start | bytes 393220
  206.7 36.8 %copy-start.14 = (f32[128,256]{1,0:T(8,128)}, f32[128,256]{1,0:T(8,128)S(1)}, u32[]{:S(2)}) copy-start(f32[128,256]{1,0:T(8,128)S(1)} %get-tuple-element.47) | copy-start | bytes 393220
  212.5 5.6 %collective-permute-start.6 = (f32[1,8,258]{2,0,1:T(1,128)S(1)}, f32[1,8,258]{2,0,1:T(1,128)S(1)}, u32[]{:S(2)}, u32[]{:S(2)}) collective-permute-start(f32[1,8,258]{2,0,1:T(1,128)S(1)} %get-tuple-element.29), channel_id=1, source_target_pairs={{1,0},{2,1},{3,2},{4,3},{5,4},{6,5},{7,6},{8,7},{9,8},{10,9},{11,1... | collective-permute-start | bytes 24776 | tf_op jit(solution)/shard_map/ppermute | solution.py:21
  213.8 4.8 collective-permute-start.7
  218.0 25.5 %copy-start.2 = (f32[128,256]{1,0:T(8,128)}, f32[128,256]{1,0:T(8,128)S(1)}, u32[]{:S(2)}) copy-start(f32[128,256]{1,0:T(8,128)S(1)} %get-tuple-element.61) | copy-start | bytes 393220
  218.0 25.5 %copy-start.4 = (f32[128,256]{1,0:T(8,128)}, f32[128,256]{1,0:T(8,128)S(1)}, u32[]{:S(2)}) copy-start(f32[128,256]{1,0:T(8,128)S(1)} %get-tuple-element.62) | copy-start | bytes 393220
  221.9 12.4 %collective-permute-start.8 = (f32[128,8,1]{2,0,1:T(8,128)S(1)}, f32[128,8,1]{2,0,1:T(8,128)S(1)}, u32[]{:S(2)}, u32[]{:S(2)}) collective-permute-start(f32[128,8,1]{2,0,1:T(8,128)S(1)} %get-tuple-element.36), channel_id=1, source_target_pairs={{16,0},{32,16},{48,32},{64,48},{80,64},{96,80},{112,96},{17,1},{33... | collective-permute-start | bytes 12296 | tf_op jit(solution)/shard_map/ppermute | solution.py:21
  223.8 11.6 %collective-permute-start.9 = (f32[128,8,1]{2,0,1:T(8,128)S(1)}, f32[128,8,1]{2,0,1:T(8,128)S(1)}, u32[]{:S(2)}, u32[]{:S(2)}) collective-permute-start(f32[128,8,1]{2,0,1:T(8,128)S(1)} %get-tuple-element.35), channel_id=1, source_target_pairs={{0,16},{16,32},{32,48},{48,64},{64,80},{80,96},{96,112},{1,17},{17... | collective-permute-start | bytes 12296 | tf_op jit(solution)/shard_map/ppermute | solution.py:20
  235.6 5.9 %collective-permute-start.10 = (f32[1,8,258]{2,0,1:T(1,128)S(1)}, f32[1,8,258]{2,0,1:T(1,128)S(1)}, u32[]{:S(2)}, u32[]{:S(2)}) collective-permute-start(f32[1,8,258]{2,0,1:T(1,128)S(1)} %get-tuple-element.25), channel_id=1, source_target_pairs={{1,0},{2,1},{3,2},{4,3},{5,4},{6,5},{7,6},{8,7},{9,8},{10,9},{11,1... | collective-permute-start | bytes 24776 | tf_op jit(solution)/shard_map/ppermute | solution.py:21
  236.9 5.4 %collective-permute-start.11 = (f32[1,8,258]{2,0,1:T(1,128)S(1)}, f32[1,8,258]{2,0,1:T(1,128)S(1)}, u32[]{:S(2)}, u32[]{:S(2)}) collective-permute-start(f32[1,8,258]{2,0,1:T(1,128)S(1)} %get-tuple-element.26), channel_id=1, source_target_pairs={{0,1},{1,2},{2,3},{3,4},{4,5},{5,6},{6,7},{7,8},{8,9},{9,10},{10,1... | collective-permute-start | bytes 24776 | tf_op jit(solution)/shard_map/ppermute | solution.py:20
  381.4 10.5 %collective-permute-start.12 = (f32[128,8,1]{2,0,1:T(8,128)S(1)}, f32[128,8,1]{2,0,1:T(8,128)S(1)}, u32[]{:S(2)}, u32[]{:S(2)}) collective-permute-start(f32[128,8,1]{2,0,1:T(8,128)S(1)} %get-tuple-element.34), channel_id=1, source_target_pairs={{16,0},{32,16},{48,32},{64,48},{80,64},{96,80},{112,96},{17,1},{33... | collective-permute-start | bytes 12296 | tf_op jit(solution)/shard_map/ppermute | solution.py:21
  383.9 9.2 %collective-permute-start.13 = (f32[128,8,1]{2,0,1:T(8,128)S(1)}, f32[128,8,1]{2,0,1:T(8,128)S(1)}, u32[]{:S(2)}, u32[]{:S(2)}) collective-permute-start(f32[128,8,1]{2,0,1:T(8,128)S(1)} %get-tuple-element.33), channel_id=1, source_target_pairs={{0,16},{16,32},{32,48},{48,64},{64,80},{80,96},{96,112},{1,17},{17... | collective-permute-start | bytes 12296 | tf_op jit(solution)/shard_map/ppermute | solution.py:20
  393.2 5.7 %collective-permute-start.14 = (f32[1,8,258]{2,0,1:T(1,128)S(1)}, f32[1,8,258]{2,0,1:T(1,128)S(1)}, u32[]{:S(2)}, u32[]{:S(2)}) collective-permute-start(f32[1,8,258]{2,0,1:T(1,128)S(1)} %get-tuple-element.21), channel_id=1, source_target_pairs={{1,0},{2,1},{3,2},{4,3},{5,4},{6,5},{7,6},{8,7},{9,8},{10,9},{11,1... | collective-permute-start | bytes 24776 | tf_op jit(solution)/shard_map/ppermute | solution.py:21
  394.5 6.2 %copy-start.3 = (f32[128,256]{1,0:T(8,128)S(1)}, f32[128,256]{1,0:T(8,128)}, u32[]{:S(2)}) copy-start(f32[128,256]{1,0:T(8,128)} %copy-done.2) | copy-start | bytes 393220
  394.5 6.2 %copy-start.5 = (f32[128,256]{1,0:T(8,128)S(1)}, f32[128,256]{1,0:T(8,128)}, u32[]{:S(2)}) copy-start(f32[128,256]{1,0:T(8,128)} %copy-done.4) | copy-start | bytes 393220
  394.5 6.2 %copy-start.7 = (f32[128,256]{1,0:T(8,128)S(1)}, f32[128,256]{1,0:T(8,128)}, u32[]{:S(2)}) copy-start(f32[128,256]{1,0:T(8,128)} %copy-done.6) | copy-start | bytes 393220
  394.6 6.2 %copy-start.9 = (f32[128,256]{1,0:T(8,128)S(1)}, f32[128,256]{1,0:T(8,128)}, u32[]{:S(2)}) copy-start(f32[128,256]{1,0:T(8,128)} %copy-done.8) | copy-start | bytes 393220
  394.6 4.9 collective-permute-start.15
  402.9 12.4 %collective-permute-start.16 = (f32[128,8,1]{2,0,1:T(8,128)S(1)}, f32[128,8,1]{2,0,1:T(8,128)S(1)}, u32[]{:S(2)}, u32[]{:S(2)}) collective-permute-start(f32[128,8,1]{2,0,1:T(8,128)S(1)} %get-tuple-element.32), channel_id=1, source_target_pairs={{16,0},{32,16},{48,32},{64,48},{80,64},{96,80},{112,96},{17,1},{33... | collective-permute-start | bytes 12296 | tf_op jit(solution)/shard_map/ppermute | solution.py:21
  404.8 11.6 %collective-permute-start.17 = (f32[128,8,1]{2,0,1:T(8,128)S(1)}, f32[128,8,1]{2,0,1:T(8,128)S(1)}, u32[]{:S(2)}, u32[]{:S(2)}) collective-permute-start(f32[128,8,1]{2,0,1:T(8,128)S(1)} %get-tuple-element.31), channel_id=1, source_target_pairs={{0,16},{16,32},{32,48},{48,64},{64,80},{80,96},{96,112},{1,17},{17... | collective-permute-start | bytes 12296 | tf_op jit(solution)/shard_map/ppermute | solution.py:20
  416.6 5.9 %collective-permute-start.18 = (f32[1,8,258]{2,0,1:T(1,128)S(1)}, f32[1,8,258]{2,0,1:T(1,128)S(1)}, u32[]{:S(2)}, u32[]{:S(2)}) collective-permute-start(f32[1,8,258]{2,0,1:T(1,128)S(1)} %get-tuple-element.17), channel_id=1, source_target_pairs={{1,0},{2,1},{3,2},{4,3},{5,4},{6,5},{7,6},{8,7},{9,8},{10,9},{11,1... | collective-permute-start | bytes 24776 | tf_op jit(solution)/shard_map/ppermute | solution.py:21
  417.9 5.4 %collective-permute-start.19 = (f32[1,8,258]{2,0,1:T(1,128)S(1)}, f32[1,8,258]{2,0,1:T(1,128)S(1)}, u32[]{:S(2)}, u32[]{:S(2)}) collective-permute-start(f32[1,8,258]{2,0,1:T(1,128)S(1)} %get-tuple-element.18), channel_id=1, source_target_pairs={{0,1},{1,2},{2,3},{3,4},{4,5},{5,6},{6,7},{7,8},{8,9},{9,10},{10,1... | collective-permute-start | bytes 24776 | tf_op jit(solution)/shard_map/ppermute | solution.py:20
  (5 other events, 21.4 us)
Sparse Core Ops, SparseCore 0:
  74.5 124.4 reduce-scatter.1
where the time goes:
time: 511 us; the launch traced here: 510 us
  blocking collectives  205 us (40%)
  waiting for transfers between devices  138 us (27%)
  matrix products  63.7 us (12%)
  starting transfers between devices  59.8 us (12%)
  other arithmetic  20.9 us (4%)
  between operations  15.3 us (3%)
  local copies, waits for them, and re-layouts  6.27 us (1%)
    psum x2, blocking collectives, squares(): return lax.psum(jnp.sum(current * current, axis=(0, 2)), ('region', 'tile'))  135 us
    reduce_scatter x1, waiting for transfers between devices, local(): lax.psum_scatter(term.reshape(rows_dev * lax.axis_size('tile'), reals + 1...  102 us
    psum x1, blocking collectives, local(): lax.psum(jnp.sum(direction * image, axis=(0, 2)), ('region', 'tile'))  70.5 us
    dot_general x1, matrix products, local(): jnp.dot(jnp.transpose(row_hot), spread, precision=lax.Precision.HIGHEST,...  63.7 us
    ppermute x10, starting transfers between devices, with_halo(): before = lax.ppermute(last, axis, up)  42.4 us
    ppermute x10, waiting for transfers between devices, with_halo(): after = lax.ppermute(leading, axis, down)  27.4 us
    ppermute x10, starting transfers between devices, with_halo(): after = lax.ppermute(leading, axis, down)  17.4 us
  transfers between devices with their start and end apart: 21, of which 16 were waited for; matrix products, arithmetic and copies ran while one was open for 0% of the time, Pallas kernels for 0%

commit v1 on v0

v1 whole, which is shorter than its diff:
```python
import jax
import jax.numpy as jnp
from jax import lax
from jax.experimental import pallas as pl
from jax.experimental.pallas import tpu as pltpu
from jax.sharding import PartitionSpec as P

PREC_SCALE = 0.01
RIM = 4
ROWS, COLS = 128, 256
REALS = 8
SLOTS = 1024
TILES, REGIONS = 16, 8
EXT = ROWS + 2 * RIM
WIDE = COLS + 128
CHUNKS = SLOTS // 128
DENSE = TILES * 128
GROUPS = 5
PIECE = EXT // 4
F32, BF16, I32 = jnp.float32, jnp.bfloat16, jnp.int32
VMEM_LIMIT = 48 * 1024 * 1024


def iota(shape, dim):
    return lax.broadcasted_iota(I32, shape, dim)


def contract_lanes(a, b):
    return lax.dot_general(a, b, (((1,), (1,)), ((), ())), preferred_element_type=F32)


def sort_body(count, cell_ref, value_ref, out):
    cell = cell_ref[...]
    index = iota((1, SLOTS), 1)
    live = index < count[0]
    key = (jnp.where(live, cell >> 8, 4096) * SLOTS + index).astype(F32)
    tall = jnp.transpose(jnp.broadcast_to(key, (128, SLOTS)))
    across = [jnp.broadcast_to(key[:, 128 * i : 128 * i + 128], (8, 128)) for i in range(CHUNKS)]
    below = [jnp.zeros((8, 128), F32) for _ in range(CHUNKS)]
    for j in range(SLOTS // 8):
        column = tall[8 * j : 8 * j + 8]
        for i in range(CHUNKS):
            below[i] = below[i] + jnp.where(column < across[i], 1.0, 0.0)
    rank = jnp.concatenate([jnp.sum(x, axis=0, keepdims=True) for x in below], axis=1).astype(I32)
    code = jnp.where(live, cell, 4096 * 256)
    value = value_ref[...]
    high = value.astype(BF16).astype(F32)
    rest = value - high
    middle = rest.astype(BF16).astype(F32)
    low = rest - middle
    left = jnp.concatenate(
        [
            high,
            middle,
            low,
            (code & 255).astype(F32),
            ((code >> 8) & 255).astype(F32),
            (code >> 16).astype(F32),
            jnp.zeros((5, SLOTS), F32),
        ],
        axis=0,
    ).astype(BF16)
    for k in range(SLOTS // 256):
        spot = jnp.where(iota((256, SLOTS), 0) + 256 * k == rank, 1.0, 0.0).astype(BF16)
        moved = contract_lanes(left, spot)
        values = (moved[0:8] + moved[8:16]) + moved[16:24]
        codes = moved[24:25] + 256.0 * moved[25:26] + 65536.0 * moved[26:27]
        for h in range(2):
            c = 2 * k + h
            out[8 * c : 8 * c + 8, :] = values[:, 128 * h : 128 * h + 128]
            out[64 + c : 65 + c, :] = codes[:, 128 * h : 128 * h + 128]


def scatter_body(recv, coef, south, north, b, w, cp, edge_l, edge_r, vals, code, ct, a, hits):
    first = lax.axis_index("tile") * ROWS - RIM
    low_cell = (first * COLS).astype(F32)
    high_cell = ((first + EXT) * COLS).astype(F32)
    cp[:, RIM : RIM + ROWS, :] = coef[...]
    cp[:, :RIM, :] = south[...]
    cp[:, RIM + ROWS :, :] = north[...]
    starts, lengths = [], []
    for s in range(TILES):
        cells = recv[s, 64:72, :]
        start = jnp.sum(jnp.where(cells < low_cell, 1.0, 0.0)).astype(I32)
        end = jnp.sum(jnp.where(cells < high_cell, 1.0, 0.0)).astype(I32)
        starts.append(start)
        lengths.append(end - start)
    most = lengths[0]
    for x in lengths[1:]:
        most = jnp.maximum(most, x)
    b[...] = jnp.zeros(b.shape, F32)
    hits[...] = jnp.zeros(hits.shape, F32)
    lane = iota((1, 128), 1)

    def one_round(k, carry):
        for s in range(TILES):
            here = jnp.minimum((starts[s] >> 7) + k, CHUNKS - 1)
            after = jnp.minimum(here + 1, CHUNKS - 1)
            shift = starts[s] & 127
            back = (128 - shift) & 127
            head = lane < 128 - shift
            inside = lane + 128 * k < lengths[s]
            v0 = pltpu.roll(recv[s, pl.ds(pl.multiple_of(here * 8, 8), 8), :], back, 1)
            v1 = pltpu.roll(recv[s, pl.ds(pl.multiple_of(after * 8, 8), 8), :], back, 1)
            c0 = pltpu.roll(jnp.broadcast_to(recv[s, pl.ds(64 + here, 1), :], (8, 128)), back, 1)
            c1 = pltpu.roll(jnp.broadcast_to(recv[s, pl.ds(64 + after, 1), :], (8, 128)), back, 1)
            value = jnp.where(inside, jnp.where(head, v0, v1), 0.0)
            local = jnp.where(head, c0, c1).astype(I32) - first * COLS
            vals[:, 128 * s : 128 * s + 128] = value
            code[:, 128 * s : 128 * s + 128] = jnp.where(inside, local, -COLS)
        row = code[...] >> 8
        column = code[0:1, :] & 255
        value = vals[...]
        high = value.astype(BF16).astype(F32)
        low = value - high
        ct[...] = jnp.where(iota((COLS, DENSE), 0) == column, 1.0, 0.0).astype(BF16)

        def piece(p, carry):
            base = p * PIECE
            for i in range(PIECE // 2):
                here = jnp.concatenate([row == base + 2 * i, row == base + 2 * i + 1], axis=0)
                both = jnp.concatenate([high, high], axis=0)
                a[16 * i : 16 * i + 16, :] = jnp.where(here, both, 0.0).astype(BF16)
                both = jnp.concatenate([low, low], axis=0)
                at = 8 * PIECE + 16 * i
                a[at : at + 16, :] = jnp.where(here, both, 0.0).astype(BF16)
            ones = jnp.where(iota((48, DENSE), 0) + base == row[0:1], 1.0, 0.0)
            a[16 * PIECE : 16 * PIECE + 48, :] = ones.astype(BF16)
            got = contract_lanes(a[...], ct[...])
            field = (got[: 8 * PIECE] + got[8 * PIECE : 16 * PIECE]) * 2.0
            b[pl.ds(base, PIECE)] += field.reshape(PIECE, REALS, COLS)
            hits[p] += got[16 * PIECE : 16 * PIECE + 40] * 2.0
            return carry

        return lax.fori_loop(0, EXT // PIECE, piece, carry)

    lax.fori_loop(0, (most + 127) >> 7, one_round, 0)

    for p in range(4):
        w[PIECE * p : PIECE * p + PIECE, :] = hits[p, 0:PIECE]
    lane8 = iota((8, 128), 1)
    for side, edge in ((0, edge_l), (1, edge_r)):
        cut = slice(0, 128) if side == 0 else slice(128, 256)
        for g in range(GROUPS):
            packed = jnp.zeros((8, 128), F32)
            packed_w = jnp.zeros((1, 128), F32)
            for j in range(min(32, EXT - 32 * g)):
                r = 32 * g + j
                turn = (4 * j + (0 if side == 0 else RIM)) % 128
                mine = (lane8 >= 4 * j) & (lane8 < 4 * j + 4)
                field, weight = b[r, :, cut], w[r : r + 1, cut]
                if turn:
                    field, weight = pltpu.roll(field, turn, 1), pltpu.roll(weight, turn, 1)
                packed = jnp.where(mine, field, packed)
                packed_w = jnp.where(mine[0:1], weight, packed_w)
            edge[8 * g : 8 * g + 8, :] = packed
            edge[40 + g : 41 + g, :] = packed_w
        edge[45:48, :] = jnp.zeros((3, 128), F32)
        keep = slice(0, RIM) if side == 0 else slice(128 - RIM, 128)
        for ch in range(4):
            turned = jnp.transpose(cp[ch, 0:128, cut])
            edge[48 + 4 * ch : 52 + 4 * ch, :] = turned[keep]
    tails = [cp[ch, 128:136, 128 * side : 128 * side + 128] for side in (0, 1) for ch in range(4)]
    turned = jnp.transpose(jnp.concatenate(tails + [jnp.zeros((64, 128), F32)], axis=0))
    edge_l[64:68, :] = turned[0:RIM]
    edge_r[64:68, :] = turned[128 - RIM : 128]
    edge_l[68:72, :] = jnp.zeros((4, 128), F32)
    edge_r[68:72, :] = jnp.zeros((4, 128), F32)


def krylov_body(b, w, cp, from_l, from_r, q_out, t_out, moments, own, b3, w3, c3, st, f, q3):
    region, tile = lax.axis_index("region"), lax.axis_index("tile")
    lane = iota((8, 128), 1)
    at_right, at_left = lane < RIM, lane >= 128 - RIM

    for ref in (b3, f, q3):
        ref[0] = jnp.zeros((REALS, WIDE), F32)
        ref[EXT + 1] = jnp.zeros((REALS, WIDE), F32)
    b3[1 : EXT + 1, :, 0:COLS] = b[...]
    w3[:, 0:COLS] = w[...]
    for r in range(EXT):
        g, j = r // 32, r % 32
        right, left = from_r[8 * g : 8 * g + 8, :], from_l[8 * g : 8 * g + 8, :]
        right_w, left_w = from_r[40 + g : 41 + g, :], from_l[40 + g : 41 + g, :]
        turn = (128 - 4 * j) % 128
        if turn:
            right, right_w = pltpu.roll(right, turn, 1), pltpu.roll(right_w, turn, 1)
        turn = (252 - 4 * j) % 128
        if turn:
            left, left_w = pltpu.roll(left, turn, 1), pltpu.roll(left_w, turn, 1)
        b3[r + 1, :, COLS:] = jnp.where(at_right, right, jnp.where(at_left, left, 0.0))
        w3[r : r + 1, COLS:] = jnp.where(
            at_right[0:1], right_w, jnp.where(at_left[0:1], left_w, 0.0)
        )
    c3[:, 0:8, :] = jnp.zeros((4, 8, WIDE), F32)
    c3[:, EXT + 8 :, :] = jnp.zeros((4, 8, WIDE), F32)
    c3[:, 8 : EXT + 8, 0:COLS] = cp[...]
    blank = jnp.zeros((128 - 2 * RIM, 128), F32)
    for ch in range(4):
        s = slice(48 + 4 * ch, 52 + 4 * ch)
        c3[ch, 8:136, COLS:] = jnp.transpose(jnp.concatenate([from_r[s], blank, from_l[s]], axis=0))
    turned = jnp.transpose(jnp.concatenate([from_r[64:68], blank, from_l[64:68]], axis=0))
    for ch in range(4):
        tail = jnp.where(at_right, turned[8 * ch : 8 * ch + 8], 0.0)
        tail = tail + jnp.where(at_left, turned[32 + 8 * ch : 40 + 8 * ch], 0.0)
        c3[ch, 136:144, COLS:] = tail

    largest = jnp.ones((8, WIDE), F32)
    for ch in range(4):
        for i in range(EXT // 8):
            largest = jnp.maximum(largest, jnp.abs(c3[ch, 8 + 8 * i : 16 + 8 * i, :]))
    scale = 1.0 / jnp.max(jnp.max(largest, axis=0, keepdims=True), axis=1, keepdims=True)
    w3[...] = w3[...] * (scale * scale)

    lane3 = iota((8, WIDE), 1)
    gx = jnp.where(lane3 >= WIDE - RIM, lane3 - WIDE, lane3) + region * COLS
    inside_x = (gx >= 0) & (gx < REGIONS * COLS) & ((lane3 < COLS + RIM) | (lane3 >= WIDE - RIM))

    def east(x):
        return pltpu.roll(x, WIDE - 1, 1)

    def west(x):
        return pltpu.roll(x, 1, 1)

    def coefficients(i, carry):
        at = 8 + 8 * i
        gy = tile * ROWS - RIM + 8 * i + iota((8, WIDE), 0)
        keep = jnp.where(inside_x & (gy >= 0) & (gy < TILES * ROWS), scale, 0.0)

        def near(ch, dy):
            if dy == 0:
                return c3[ch, pl.ds(pl.multiple_of(at, 8), 8), :]
            if dy == 1:
                ahead = c3[ch, pl.ds(pl.multiple_of(at + 8, 8), 8), :]
                return jnp.concatenate([near(ch, 0)[1:8], ahead[0:1]], axis=0)
            behind = c3[ch, pl.ds(pl.multiple_of(at - 8, 8), 8), :]
            return jnp.concatenate([behind[7:8], near(ch, 0)[0:7]], axis=0)

        h11, h22, kappa = near(0, 0), near(1, 0), near(3, 0)
        e = 0.5 * (east(h11) + h11)
        wst = 0.5 * (west(h11) + h11)
        n = 0.5 * (near(1, 1) + h22)
        s = 0.5 * (near(1, -1) + h22)
        m = near(2, 0)
        me, mw, mn, ms = east(m), west(m), near(2, 1), near(2, -1)
        rows = pl.ds(pl.multiple_of(8 * i, 8), 8)
        st[0, rows, :] = keep * (kappa + ((e + wst) + (n + s)))
        st[1, rows, :] = -keep * e
        st[2, rows, :] = -keep * wst
        st[3, rows, :] = -keep * n
        st[4, rows, :] = -keep * s
        quarter = 0.25 * keep
        st[5, rows, :] = -quarter * (me + mn)
        st[6, rows, :] = quarter * (mw + mn)
        st[7, rows, :] = quarter * (me + ms)
        st[8, rows, :] = -quarter * (mw + ms)
        return carry

    lax.fori_loop(0, EXT // 8, coefficients, 0)

    def three(ref, r):
        x = ref[r + 1]
        return x, east(x), west(x)

    def apply(src, start, count, put):
        def block(i, carry):
            below, here = carry
            for d in range(8):
                r = start + 8 * i + d
                above = three(src, r + 1)
                c = [st[k, pl.ds(r, 1), :] for k in range(9)]
                total = c[0] * here[0] + c[1] * here[1] + c[2] * here[2]
                total = total + (c[3] * above[0] + c[5] * above[1] + c[6] * above[2])
                total = total + (c[4] * below[0] + c[7] * below[1] + c[8] * below[2])
                put(r, total)
                below, here = here, above
            return below, here

        lax.fori_loop(0, count, block, (three(src, start - 1), three(src, start)))

    def put_f(r, total):
        f[r + 1] = total

    def put_q(r, total):
        value = PREC_SCALE * total + w3[pl.ds(r, 1), :] * b3[r + 1]
        q3[r + 1] = value

    def put_t(r, total):
        value = PREC_SCALE * total[:, :COLS] + w3[pl.ds(r, 1), 0:COLS] * q3[r + 1, :, 0:COLS]
        t_out[r - RIM] = value
        q_out[r - RIM] = q3[r + 1, :, 0:COLS]

    apply(b3, 0, EXT // 8, put_f)
    apply(f, 0, EXT // 8, put_q)
    apply(q3, 0, EXT // 8, put_f)
    apply(f, RIM, ROWS // 8, put_t)

    zero = jnp.zeros((REALS, COLS), F32)

    def first(i, acc):
        bb, bq, bt = acc
        for d in range(8):
            r = 8 * i + d
            x = b[r + RIM]
            bb, bq, bt = bb + x * x, bq + x * q_out[r], bt + x * t_out[r]
        return bb, bq, bt

    def total(x):
        return jnp.sum(x, axis=1, keepdims=True)

    bb, bq, bt = [total(x) for x in lax.fori_loop(0, ROWS // 8, first, (zero, zero, zero))]
    safe = jnp.where(bb > 0.0, bb, 1.0)
    sigma, tau = bq / safe, bt / safe

    def second(i, acc):
        uu, uz = acc
        for d in range(8):
            r = 8 * i + d
            x = b[r + RIM]
            u = q_out[r] - sigma * x
            uu, uz = uu + u * u, uz + u * (t_out[r] - tau * x)
        return uu, uz

    uu, uz = [total(x) for x in lax.fori_loop(0, ROWS // 8, second, (zero, zero))]
    mu = uz / jnp.where(uu > 0.0, uu, 1.0)
    inverse = 1.0 / (scale * scale)
    own[...] = jnp.broadcast_to(inverse, (8, 128))
    column = [jnp.broadcast_to(x, (8, 128)) for x in (bb, sigma, uu, tau, mu, inverse)]
    moments[...] = jnp.transpose(jnp.concatenate(column + [jnp.zeros((80, 128), F32)], axis=0))


def finish_body(moments, own, b, q, t, x_out, r_out):
    turned = jnp.transpose(moments[...])
    bb, sigma, uu, tau, mu, inverse = [turned[8 * m : 8 * m + 8] for m in range(6)]

    def total(x):
        return jnp.sum(x, axis=1, keepdims=True)

    norm0 = total(bb)
    alpha0 = norm0 / total(bb * sigma * inverse)
    a = alpha0 * inverse
    off = 1.0 - a * sigma
    norm1 = total(off * off * bb + a * a * uu)
    beta = norm1 / norm0
    grow = 1.0 + beta
    along = (grow - a * sigma) * (grow * sigma - a * tau) * bb
    curve = total(inverse * (along - a * (grow - a * mu) * uu))
    alpha1 = norm1 / curve
    mine = own[:, 0:1]
    a0 = alpha0 * mine
    a1 = alpha1 * mine

    def block(i, carry):
        for d in range(8):
            r = 8 * i + d
            x, y, z = b[r + RIM], q[r], t[r]
            r1 = x - a0 * y
            d1 = r1 + beta * x
            x_out[r] = alpha0 * x + alpha1 * d1
            r_out[r] = r1 - a1 * (grow * y - a0 * z)
        return carry

    lax.fori_loop(0, ROWS // 8, block, 0)


def call(body, shapes, scratch, *args, smem=0):
    vmem = pl.BlockSpec(memory_space=pltpu.VMEM)
    return pl.pallas_call(
        body,
        out_shape=[jax.ShapeDtypeStruct(s, F32) for s in shapes],
        in_specs=[pl.BlockSpec(memory_space=pltpu.SMEM)] * smem + [vmem] * (len(args) - smem),
        out_specs=[vmem] * len(shapes),
        scratch_shapes=scratch,
        compiler_params=pltpu.CompilerParams(vmem_limit_bytes=VMEM_LIMIT),
    )(*args)


def local(coeffs, obs_cell, obs_value, obs_count):
    up_tile = [(i, i + 1) for i in range(TILES - 1)]
    down_tile = [(j, i) for i, j in up_tile]
    up_region = [(i, i + 1) for i in range(REGIONS - 1)]
    down_region = [(j, i) for i, j in up_region]
    south = lax.ppermute(coeffs[:, ROWS - RIM :, :], "tile", up_tile)
    north = lax.ppermute(coeffs[:, :RIM, :], "tile", down_tile)
    (packed,) = call(
        sort_body, [(72, 128)], [], obs_count, obs_cell.reshape(1, SLOTS), obs_value, smem=1
    )
    recv = lax.all_to_all(jnp.broadcast_to(packed[None], (TILES, 72, 128)), "tile", 0, 0)
    b, w, cp, edge_l, edge_r = call(
        scatter_body,
        [(EXT, REALS, COLS), (EXT, COLS), (4, EXT, COLS), (72, 128), (72, 128)],
        [
            pltpu.VMEM((REALS, DENSE), F32),
            pltpu.VMEM((REALS, DENSE), I32),
            pltpu.VMEM((COLS, DENSE), BF16),
            pltpu.VMEM((16 * PIECE + 48, DENSE), BF16),
            pltpu.VMEM((4, 40, COLS), F32),
        ],
        recv,
        coeffs,
        south,
        north,
    )
    from_l = lax.ppermute(edge_r, "region", up_region)
    from_r = lax.ppermute(edge_l, "region", down_region)
    field = (ROWS, REALS, COLS)
    q, t, moments, own = call(
        krylov_body,
        [field, field, (128, 128), (8, 128)],
        [
            pltpu.VMEM((EXT + 2, REALS, WIDE), F32),
            pltpu.VMEM((EXT, WIDE), F32),
            pltpu.VMEM((4, EXT + 16, WIDE), F32),
            pltpu.VMEM((9, EXT, WIDE), F32),
            pltpu.VMEM((EXT + 2, REALS, WIDE), F32),
            pltpu.VMEM((EXT + 2, REALS, WIDE), F32),
        ],
        b,
        w,
        cp,
        from_l,
        from_r,
    )
    shared = lax.all_to_all(moments, ("region", "tile"), 0, 0, tiled=True)
    return tuple(call(finish_body, [field, field], [], shared, own, b, q, t))


def solution(mesh):
    placed = (
        P(None, "tile", "region"),
        P(("region", "tile")),
        P(None, ("region", "tile")),
        P(("region", "tile")),
    )
    return jax.shard_map(
        local,
        mesh=mesh,
        in_specs=placed,
        out_specs=(P("tile", None, "region"), P("tile", None, "region")),
        check_vma=False,
    )
```

time: 511 us -> 72.6 us (0.14)
  blocking collectives: 205 us -> 16.3 us
  waiting for transfers between devices: 138 us -> 9.09 us
  matrix products: 63.7 us -> 0 us
  starting transfers between devices: 59.8 us -> 21 us
  Pallas kernels: 0 us -> 22.1 us
  other arithmetic: 20.9 us -> 0 us
  between operations: 15.3 us -> 1.43 us
    psum x3 -> x0, blocking collectives: 205 us -> none  [the longest x2 135 us: squares(): return lax.psum(jnp.sum(current * current, axis=(0, 2)), ('region', 'tile'))]
    reduce_scatter x1 -> x0, waiting for transfers between devices: 102 us -> none  [local(): lax.psum_scatter(term.reshape(rows_dev * lax.axis_size('tile'), reals + 1...]
    dot_general x1 -> x0, matrix products: 63.7 us -> none  [local(): jnp.dot(jnp.transpose(row_hot), spread, precision=lax.Precision.HIGHEST,...]
    ppermute x20 -> x4, starting transfers between devices: 59.8 us -> 12.6 us  [the longest x1 5.38 us: local(): from_l = lax.ppermute(edge_r, 'region', up_region)]
    ppermute x20 -> x4, waiting for transfers between devices: 36.1 us -> 6.12 us  [the longest x1 3.34 us: local(): from_r = lax.ppermute(edge_l, 'region', down_region)]
    pallas_call x0 -> x4, Pallas kernels: none -> 22.1 us  [call(): pl.pallas_call(body, out_shape=[jax.ShapeDtypeStruct(s, F32) for s in sha...]
    all_to_all x0 -> x1, blocking collectives: none -> 16.3 us  [local(): shared = lax.all_to_all(moments, ('region', 'tile'), 0, 0, tiled=True)]
    all_to_all x0 -> x1, starting transfers between devices: none -> 8.43 us  [local(): lax.all_to_all(jnp.broadcast_to(packed[None], (TILES, 72, 128)), 'tile',...]
  transfers between devices with their start and end apart: 21 -> 5, of which waited for: 16 -> 3; matrix products, arithmetic and copies ran while one was open for 0% -> 0% of each run, Pallas kernels for 0% -> 0%
where the time goes in v1:
time: 72.6 us; the launch traced here: 72.2 us
  Pallas kernels  22.1 us (30%)
  starting transfers between devices  21 us (29%)
  blocking collectives  16.3 us (22%)
  waiting for transfers between devices  9.09 us (13%)
  local copies, waits for them, and re-layouts  2.3 us (3%)
  between operations  1.43 us (2%)
    pallas_call x4, Pallas kernels, call(): pl.pallas_call(body, out_shape=[jax.ShapeDtypeStruct(s, F32) for s in sha...  22.1 us
    all_to_all x1, blocking collectives, local(): shared = lax.all_to_all(moments, ('region', 'tile'), 0, 0, tiled=True)  16.3 us
    all_to_all x1, starting transfers between devices, local(): lax.all_to_all(jnp.broadcast_to(packed[None], (TILES, 72, 128)), 'tile',...  8.43 us
    ppermute x1, starting transfers between devices, local(): from_l = lax.ppermute(edge_r, 'region', up_region)  5.38 us
    ppermute x1, starting transfers between devices, local(): south = lax.ppermute(coeffs[:, ROWS - RIM:, :], 'tile', up_tile)  3.99 us
    ppermute x1, waiting for transfers between devices, local(): from_r = lax.ppermute(edge_l, 'region', down_region)  3.34 us
    all_to_all x1, waiting for transfers between devices, local(): lax.all_to_all(jnp.broadcast_to(packed[None], (TILES, 72, 128)), 'tile',...  2.96 us
    ppermute x1, waiting for transfers between devices, local(): north = lax.ppermute(coeffs[:, :RIM, :], 'tile', down_tile)  2.78 us
  transfers between devices with their start and end apart: 5, of which 3 were waited for; matrix products, arithmetic and copies ran while one was open for 0% of the time, Pallas kernels for 0%

profile of v1, /device:TPU:1, one launch (start us, length us, event | category | flops | bytes accessed | tf_op | source)
XLA Modules:
  0.0 72.2 jit_solution(1393697270227994160)
XLA Ops:
  0.6 0.0 copy-start
  1.3 0.0 copy-start.1
  1.4 0.7 %copy-done.1 = f32[8,1024]{1,0:T(8,128)S(1)} copy-done((f32[8,1024]{1,0:T(8,128)S(1)}, f32[8,1024]{1,0:T(8,128)}, u32[]{:S(2)}) %copy-start.1) | copy-done | bytes 32792
  2.1 0.0 copy-start.2
  2.1 0.7 copy-done.2
  2.8 1.2 %shard_map.59 = f32[72,128]{1,0:T(8,128)S(1)} custom-call(s32[1]{0:T(128)S(6)} %copy.7.count, s32[1,1024]{1,0:T(1,128)S(1)} %bitcast.7, f32[8,1024]{1,0:T(8,128)S(1)} %copy-done.1), custom_call_target="tpu_custom_call" | custom-call | tf_op jit(solution)/shard_map/pallas_call | solution.py:368
  4.0 0.9 %broadcast_in_dim.2 = f32[16,72,128]{2,1,0:T(8,128)} broadcast(f32[72,128]{1,0:T(8,128)S(1)} %shard_map.59), dimensions={1,2} | broadcast | bytes 626688 | tf_op jit(solution)/shard_map/broadcast_in_dim | solution.py:388
  4.9 8.4 %all-to-all-start = ((f32[16,72,128]{2,1,0:T(8,128)}), f32[16,72,128]{2,1,0:T(8,128)S(1)}, u32[]{:S(2)}, u32[]{:S(2)}) async-start(f32[16,72,128]{2,1,0:T(8,128)} %broadcast_in_dim.2), calls=%async_computation | async-start | bytes 1179648 | tf_op jit(solution)/shard_map/all_to_all | solution.py:388
  13.3 0.0 copy-done
  13.3 1.3 %collective-permute-start.1 = (f32[4,4,256]{2,1,0:T(4,128)S(1)}, f32[4,4,256]{2,1,0:T(4,128)S(1)}, u32[]{:S(2)}, u32[]{:S(2)}) collective-permute-start(f32[4,4,256]{2,1,0:T(4,128)S(1)} %get-tuple-element.20), channel_id=1, source_target_pairs={{1,0},{2,1},{3,2},{4,3},{5,4},{6,5},{7,6},{8,7},{9,8},{10,9},{11,1... | collective-permute-start | bytes 49160 | tf_op jit(solution)/shard_map/ppermute | solution.py:384
  14.6 4.0 %collective-permute-start = (f32[4,4,256]{2,1,0:T(4,128)S(1)}, f32[4,4,256]{2,1,0:T(4,128)S(1)}, u32[]{:S(2)}, u32[]{:S(2)}) collective-permute-start(f32[4,4,256]{2,1,0:T(4,128)S(1)} %get-tuple-element.21), channel_id=1, source_target_pairs={{0,1},{1,2},{2,3},{3,4},{4,5},{5,6},{6,7},{7,8},{8,9},{9,10},{10,1... | collective-permute-start | bytes 49160 | tf_op jit(solution)/shard_map/ppermute | solution.py:383
  18.6 2.8 %collective-permute-done.1.north = f32[4,4,256]{2,1,0:T(4,128)S(1)} collective-permute-done((f32[4,4,256]{2,1,0:T(4,128)S(1)}, f32[4,4,256]{2,1,0:T(4,128)S(1)}, u32[]{:S(2)}, u32[]{:S(2)}) %collective-permute-start.1) | collective-permute-done | bytes 16416 | tf_op jit(solution)/shard_map/ppermute | solution.py:384
  21.4 0.0 collective-permute-done.south
  21.4 3.0 %all-to-all-done.recv = f32[16,72,128]{2,1,0:T(8,128)S(1)} async-done(((f32[16,72,128]{2,1,0:T(8,128)}), f32[16,72,128]{2,1,0:T(8,128)S(1)}, u32[]{:S(2)}, u32[]{:S(2)}) %all-to-all-start) | async-done | bytes 589856 | tf_op jit(solution)/shard_map/all_to_all | solution.py:388
  24.4 5.0 %shard_map.60 = (f32[136,8,256]{2,1,0:T(8,128)S(1)}, f32[136,256]{1,0:T(8,128)S(1)}, f32[4,136,256]{2,1,0:T(8,128)S(1)}, f32[72,128]{1,0:T(8,128)S(1)}, f32[72,128]{1,0:T(8,128)S(1)}) custom-call(f32[16,72,128]{2,1,0:T(8,128)S(1)} %all-to-all-done.recv, f32[4,128,256]{2,1,0:T(8,128)S(1)} %copy-done, f32[4,4,256]{2,1,0:T(4,128)S(1)} %collective-permute-done.south, ...), custom_call_target="tpu_custom_call" | custom-call | tf_op jit(solution)/shard_map/pallas_call | solution.py:368
  29.3 5.4 %collective-permute-start.2 = (f32[72,128]{1,0:T(8,128)S(1)}, f32[72,128]{1,0:T(8,128)S(1)}, u32[]{:S(2)}, u32[]{:S(2)}) collective-permute-start(f32[72,128]{1,0:T(8,128)S(1)} %get-tuple-element.14), channel_id=1, source_target_pairs={{0,16},{16,32},{32,48},{48,64},{64,80},{80,96},{96,112},{1,17},{17... | collective-permute-start | bytes 110600 | tf_op jit(solution)/shard_map/ppermute | solution.py:404
  34.7 1.9 %collective-permute-start.3 = (f32[72,128]{1,0:T(8,128)S(1)}, f32[72,128]{1,0:T(8,128)S(1)}, u32[]{:S(2)}, u32[]{:S(2)}) collective-permute-start(f32[72,128]{1,0:T(8,128)S(1)} %get-tuple-element.15), channel_id=1, source_target_pairs={{16,0},{32,16},{48,32},{64,48},{80,64},{96,80},{112,96},{17,1},{33... | collective-permute-start | bytes 110600 | tf_op jit(solution)/shard_map/ppermute | solution.py:405
  36.7 0.0 collective-permute-done.2.from_l
  36.7 3.3 %collective-permute-done.3.from_r = f32[72,128]{1,0:T(8,128)S(1)} collective-permute-done((f32[72,128]{1,0:T(8,128)S(1)}, f32[72,128]{1,0:T(8,128)S(1)}, u32[]{:S(2)}, u32[]{:S(2)}) %collective-permute-start.3) | collective-permute-done | bytes 36896 | tf_op jit(solution)/shard_map/ppermute | solution.py:405
  40.0 12.8 %shard_map.61 = (f32[128,8,256]{2,1,0:T(8,128)S(1)}, f32[128,8,256]{2,1,0:T(8,128)S(1)}, f32[128,128]{1,0:T(8,128)S(1)}, f32[8,128]{1,0:T(8,128)S(1)}) custom-call(f32[136,8,256]{2,1,0:T(8,128)S(1)} %get-tuple-element.11.b, f32[136,256]{1,0:T(8,128)S(1)} %get-tuple-element.12.w, f32[4,136,256]{2,1,0:T(8,128)S(1)} %get-tuple-element.13.cp, ...), custom_call_target="tpu_custom_call" | custom-call | tf_op jit(solution)/shard_map/pallas_call | solution.py:368
  52.8 16.3 %all_to_all.16 = f32[128,1,128]{2,1,0:T(1,128)S(1)} all-to-all(f32[128,1,128]{2,1,0:T(1,128)S(1)} %bitcast.6), channel_id=1, replica_groups=mesh['region'=8,'tile'=16] {'region','tile'}, dimensions={0} | all-to-all | bytes 131072 | tf_op jit(solution)/shard_map/all_to_all | solution.py:424
  69.1 3.1 %shard_map.62 = (f32[128,8,256]{2,1,0:T(8,128)}, f32[128,8,256]{2,1,0:T(8,128)}) custom-call(f32[128,128]{1,0:T(8,128)S(1)} %bitcast.5, f32[8,128]{1,0:T(8,128)S(1)} %get-tuple-element.17.own, f32[136,8,256]{2,1,0:T(8,128)S(1)} %get-tuple-element.11.b, f32[128,8,256]{2,1,0:T(8,128)S(1)} %get-tuple-element.18.q, f32[128,8,256]{2,1,0:T(8,128)S(1)} %get-tuple-element.19.t), custom_call_target="tpu_custom_call" | custom-call | tf_op jit(solution)/shard_map/pallas_call | solution.py:368
  (1 shorter events, 0.0 us)
Async XLA Ops:
  0.6 12.7 %copy-start = (f32[4,128,256]{2,1,0:T(8,128)S(1)}, f32[4,128,256]{2,1,0:T(8,128)}, u32[]{:S(2)}) copy-start(f32[4,128,256]{2,1,0:T(8,128)} %coef.1) | copy-start | bytes 1572868
  1.3 0.8 %copy-start.1 = (f32[8,1024]{1,0:T(8,128)S(1)}, f32[8,1024]{1,0:T(8,128)}, u32[]{:S(2)}) copy-start(f32[8,1024]{1,0:T(8,128)} %value_ref.1) | copy-start | bytes 98308
  2.1 0.7 copy-start.2
  4.9 19.5 %all-to-all-start = ((f32[16,72,128]{2,1,0:T(8,128)}), f32[16,72,128]{2,1,0:T(8,128)S(1)}, u32[]{:S(2)}, u32[]{:S(2)}) async-start(f32[16,72,128]{2,1,0:T(8,128)} %broadcast_in_dim.2), calls=%async_computation | async-start | bytes 1179648 | tf_op jit(solution)/shard_map/all_to_all | solution.py:388
  13.3 8.1 %collective-permute-start.1 = (f32[4,4,256]{2,1,0:T(4,128)S(1)}, f32[4,4,256]{2,1,0:T(4,128)S(1)}, u32[]{:S(2)}, u32[]{:S(2)}) collective-permute-start(f32[4,4,256]{2,1,0:T(4,128)S(1)} %get-tuple-element.20), channel_id=1, source_target_pairs={{1,0},{2,1},{3,2},{4,3},{5,4},{6,5},{7,6},{8,7},{9,8},{10,9},{11,1... | collective-permute-start | bytes 49160 | tf_op jit(solution)/shard_map/ppermute | solution.py:384
  14.6 6.8 %collective-permute-start = (f32[4,4,256]{2,1,0:T(4,128)S(1)}, f32[4,4,256]{2,1,0:T(4,128)S(1)}, u32[]{:S(2)}, u32[]{:S(2)}) collective-permute-start(f32[4,4,256]{2,1,0:T(4,128)S(1)} %get-tuple-element.21), channel_id=1, source_target_pairs={{0,1},{1,2},{2,3},{3,4},{4,5},{5,6},{6,7},{7,8},{8,9},{9,10},{10,1... | collective-permute-start | bytes 49160 | tf_op jit(solution)/shard_map/ppermute | solution.py:383
  29.3 7.3 %collective-permute-start.2 = (f32[72,128]{1,0:T(8,128)S(1)}, f32[72,128]{1,0:T(8,128)S(1)}, u32[]{:S(2)}, u32[]{:S(2)}) collective-permute-start(f32[72,128]{1,0:T(8,128)S(1)} %get-tuple-element.14), channel_id=1, source_target_pairs={{0,16},{16,32},{32,48},{48,64},{64,80},{80,96},{96,112},{1,17},{17... | collective-permute-start | bytes 110600 | tf_op jit(solution)/shard_map/ppermute | solution.py:404
  34.7 5.3 %collective-permute-start.3 = (f32[72,128]{1,0:T(8,128)S(1)}, f32[72,128]{1,0:T(8,128)S(1)}, u32[]{:S(2)}, u32[]{:S(2)}) collective-permute-start(f32[72,128]{1,0:T(8,128)S(1)} %get-tuple-element.15), channel_id=1, source_target_pairs={{16,0},{32,16},{48,32},{64,48},{80,64},{96,80},{112,96},{17,1},{33... | collective-permute-start | bytes 110600 | tf_op jit(solution)/shard_map/ppermute | solution.py:405

commit v2 on v1

v2 whole, which is shorter than its diff:
```python
import jax
import jax.numpy as jnp
from jax import lax
from jax.experimental import pallas as pl
from jax.experimental.pallas import tpu as pltpu
from jax.sharding import PartitionSpec as P

PREC_SCALE = 0.01
RIM = 4
ROWS, COLS = 128, 256
REALS = 8
SLOTS = 1024
TILES, REGIONS = 16, 8
EXT = ROWS + 2 * RIM
WIDE = COLS + 128
CHUNKS = SLOTS // 128
SHARE = 96
DENSE = TILES * SHARE
GROUPS = 5
PART = 16
PIECE = EXT // 4
F32, BF16, I32 = jnp.float32, jnp.bfloat16, jnp.int32
VMEM_LIMIT = 48 * 1024 * 1024


def iota(shape, dim):
    return lax.broadcasted_iota(I32, shape, dim)


def contract_lanes(a, b):
    return lax.dot_general(a, b, (((1,), (1,)), ((), ())), preferred_element_type=F32)


def sort_body(count, cell_hbm, value_hbm, out, cell_ref, value_ref, arrive):
    copies = [
        pltpu.make_async_copy(cell_hbm, cell_ref, arrive.at[0]),
        pltpu.make_async_copy(value_hbm, value_ref, arrive.at[1]),
    ]
    for c in copies:
        c.start()
    copies[0].wait()
    cell = cell_ref[...]
    index = iota((1, SLOTS), 1)
    live = index < count[0]
    key = (jnp.where(live, cell >> 8, 4096) * SLOTS + index).astype(F32)
    tall = jnp.transpose(jnp.broadcast_to(key, (128, SLOTS)))
    across = [jnp.broadcast_to(key[:, 128 * i : 128 * i + 128], (8, 128)) for i in range(CHUNKS)]
    below = [jnp.zeros((8, 128), F32) for _ in range(CHUNKS)]
    for j in range(SLOTS // 8):
        column = tall[8 * j : 8 * j + 8]
        for i in range(CHUNKS):
            below[i] = below[i] + jnp.where(column < across[i], 1.0, 0.0)
    rank = jnp.concatenate([jnp.sum(x, axis=0, keepdims=True) for x in below], axis=1).astype(I32)
    code = jnp.where(live, cell, 4096 * 256)
    copies[1].wait()
    value = value_ref[...]
    high = value.astype(BF16).astype(F32)
    rest = value - high
    middle = rest.astype(BF16).astype(F32)
    low = rest - middle
    left = jnp.concatenate(
        [
            high,
            middle,
            low,
            (code & 255).astype(F32),
            ((code >> 8) & 255).astype(F32),
            (code >> 16).astype(F32),
            jnp.zeros((5, SLOTS), F32),
        ],
        axis=0,
    ).astype(BF16)
    for k in range(SLOTS // 256):
        spot = jnp.where(iota((256, SLOTS), 0) + 256 * k == rank, 1.0, 0.0).astype(BF16)
        moved = contract_lanes(left, spot)
        values = (moved[0:8] + moved[8:16]) + moved[16:24]
        codes = moved[24:25] + 256.0 * moved[25:26] + 65536.0 * moved[26:27]
        for h in range(2):
            c = 2 * k + h
            for s in range(TILES):
                out[s, 8 * c : 8 * c + 8, :] = values[:, 128 * h : 128 * h + 128]
                out[s, 64 + c : 65 + c, :] = codes[:, 128 * h : 128 * h + 128]


def scatter_body(recv, coef, south, north, b, w, cp, edge_l, edge_r, vals, code, ct, a, hits):
    first = lax.axis_index("tile") * ROWS - RIM
    low_cell = (first * COLS).astype(F32)
    high_cell = ((first + EXT) * COLS).astype(F32)
    cp[:, RIM : RIM + ROWS, :] = coef[...]
    tile = lax.axis_index("tile")
    cp[:, :RIM, :] = jnp.where(tile == 0, 0.0, south[...])
    cp[:, RIM + ROWS :, :] = jnp.where(tile == TILES - 1, 0.0, north[...])
    starts, lengths = [], []
    for s in range(TILES):
        cells = recv[s, 64:72, :]
        start = jnp.sum(jnp.where(cells < low_cell, 1.0, 0.0)).astype(I32)
        end = jnp.sum(jnp.where(cells < high_cell, 1.0, 0.0)).astype(I32)
        starts.append(start)
        lengths.append(end - start)
    most = lengths[0]
    for x in lengths[1:]:
        most = jnp.maximum(most, x)
    b[...] = jnp.zeros(b.shape, F32)
    hits[...] = jnp.zeros(hits.shape, F32)
    lane = iota((1, 128), 1)

    def one_round(k, carry):
        for chunk in range(DENSE // 128):
            value, local = jnp.zeros((REALS, 128), F32), jnp.full((8, 128), -COLS, I32)
            for s in range(128 * chunk // SHARE, (128 * chunk + 127) // SHARE + 1):
                begin = starts[s] + SHARE * k
                here = jnp.minimum(begin >> 7, CHUNKS - 1)
                after = jnp.minimum(here + 1, CHUNKS - 1)
                at = begin & 127
                offset = SHARE * s - 128 * chunk
                turn = (offset - at) & 127
                spot = lane - offset
                head = spot < 128 - at
                inside = (spot >= 0) & (spot < SHARE) & (spot + SHARE * k < lengths[s])
                v0 = pltpu.roll(recv[s, pl.ds(pl.multiple_of(here * 8, 8), 8), :], turn, 1)
                v1 = pltpu.roll(recv[s, pl.ds(pl.multiple_of(after * 8, 8), 8), :], turn, 1)
                c0 = jnp.broadcast_to(recv[s, pl.ds(64 + here, 1), :], (8, 128))
                c1 = jnp.broadcast_to(recv[s, pl.ds(64 + after, 1), :], (8, 128))
                c0, c1 = pltpu.roll(c0, turn, 1), pltpu.roll(c1, turn, 1)
                value = jnp.where(inside, jnp.where(head, v0, v1), value)
                cells = jnp.where(head, c0, c1).astype(I32) - first * COLS
                local = jnp.where(inside, cells, local)
            vals[:, 128 * chunk : 128 * chunk + 128] = value
            code[:, 128 * chunk : 128 * chunk + 128] = local
        row = code[...] >> 8
        column = code[0:1, :] & 255
        value = vals[...]
        high = value.astype(BF16).astype(F32)
        low = value - high
        ct[...] = jnp.where(iota((COLS, DENSE), 0) == column, 1.0, 0.0).astype(BF16)

        for p in range(4):
            base = p * PIECE
            for i in range(PIECE // 2):
                here = jnp.concatenate([row == base + 2 * i, row == base + 2 * i + 1], axis=0)
                both = jnp.concatenate([high, high], axis=0)
                a[p, 16 * i : 16 * i + 16, :] = jnp.where(here, both, 0.0).astype(BF16)
                both = jnp.concatenate([low, low], axis=0)
                at = 8 * PIECE + 16 * i
                a[p, at : at + 16, :] = jnp.where(here, both, 0.0).astype(BF16)
            ones = jnp.where(iota((48, DENSE), 0) + base == row[0:1], 1.0, 0.0)
            a[p, 16 * PIECE : 16 * PIECE + 48, :] = ones.astype(BF16)
            got = contract_lanes(a[p], ct[...])
            field = (got[: 8 * PIECE] + got[8 * PIECE : 16 * PIECE]) * 2.0
            b[base : base + PIECE] += field.reshape(PIECE, REALS, COLS)
            hits[p] += got[16 * PIECE : 16 * PIECE + 40] * 2.0
        return carry

    lax.fori_loop(0, (most + SHARE - 1) // SHARE, one_round, 0)

    for p in range(4):
        w[PIECE * p : PIECE * p + PIECE, :] = hits[p, 0:PIECE]
    lane8 = iota((8, 128), 1)
    for side, edge in ((0, edge_l), (1, edge_r)):
        cut = slice(0, 128) if side == 0 else slice(128, 256)
        for g in range(GROUPS):
            packed = jnp.zeros((8, 128), F32)
            packed_w = jnp.zeros((1, 128), F32)
            for j in range(min(32, EXT - 32 * g)):
                r = 32 * g + j
                turn = (4 * j + (0 if side == 0 else RIM)) % 128
                mine = (lane8 >= 4 * j) & (lane8 < 4 * j + 4)
                field, weight = b[r, :, cut], w[r : r + 1, cut]
                if turn:
                    field, weight = pltpu.roll(field, turn, 1), pltpu.roll(weight, turn, 1)
                packed = jnp.where(mine, field, packed)
                packed_w = jnp.where(mine[0:1], weight, packed_w)
            edge[8 * g : 8 * g + 8, :] = packed
            edge[40 + g : 41 + g, :] = packed_w
        edge[45:48, :] = jnp.zeros((3, 128), F32)
        keep = slice(0, RIM) if side == 0 else slice(128 - RIM, 128)
        for ch in range(4):
            turned = jnp.transpose(cp[ch, 0:128, cut])
            edge[48 + 4 * ch : 52 + 4 * ch, :] = turned[keep]
    tails = [cp[ch, 128:136, 128 * side : 128 * side + 128] for side in (0, 1) for ch in range(4)]
    turned = jnp.transpose(jnp.concatenate(tails + [jnp.zeros((64, 128), F32)], axis=0))
    edge_l[64:68, :] = turned[0:RIM]
    edge_r[64:68, :] = turned[128 - RIM : 128]
    edge_l[68:72, :] = jnp.zeros((4, 128), F32)
    edge_r[68:72, :] = jnp.zeros((4, 128), F32)


def krylov_body(b, w, cp, got_l, got_r, q_out, t_out, moments, own, b3, w3, c3, st, f, q3, from_l, from_r):
    region, tile = lax.axis_index("region"), lax.axis_index("tile")
    from_l[...] = jnp.where(region == 0, 0.0, got_l[...])
    from_r[...] = jnp.where(region == REGIONS - 1, 0.0, got_r[...])
    lane = iota((8, 128), 1)
    at_right, at_left = lane < RIM, lane >= 128 - RIM

    for ref in (b3, f, q3):
        ref[0] = jnp.zeros((REALS, WIDE), F32)
        ref[EXT + 1] = jnp.zeros((REALS, WIDE), F32)

    def east(x):
        return pltpu.roll(x, WIDE - 1, 1)

    def west(x):
        return pltpu.roll(x, 1, 1)

    w3[:, 0:COLS] = w[...]
    for r in range(EXT):
        g, j = r // 32, r % 32
        right, left = from_r[8 * g : 8 * g + 8, :], from_l[8 * g : 8 * g + 8, :]
        right_w, left_w = from_r[40 + g : 41 + g, :], from_l[40 + g : 41 + g, :]
        turn = (128 - 4 * j) % 128
        if turn:
            right, right_w = pltpu.roll(right, turn, 1), pltpu.roll(right_w, turn, 1)
        turn = (252 - 4 * j) % 128
        if turn:
            left, left_w = pltpu.roll(left, turn, 1), pltpu.roll(left_w, turn, 1)
        rim = jnp.where(at_right, right, jnp.where(at_left, left, 0.0))
        b3[r + 1, :, 0:COLS] = b[r]
        b3[r + 1, :, COLS:] = rim
        w3[r : r + 1, COLS:] = jnp.where(
            at_right[0:1], right_w, jnp.where(at_left[0:1], left_w, 0.0)
        )
    c3[:, 0:8, :] = jnp.zeros((4, 8, WIDE), F32)
    c3[:, EXT + 8 :, :] = jnp.zeros((4, 8, WIDE), F32)
    c3[:, 8 : EXT + 8, 0:COLS] = cp[...]
    blank = jnp.zeros((128 - 2 * RIM, 128), F32)
    for ch in range(4):
        s = slice(48 + 4 * ch, 52 + 4 * ch)
        c3[ch, 8:136, COLS:] = jnp.transpose(jnp.concatenate([from_r[s], blank, from_l[s]], axis=0))
    turned = jnp.transpose(jnp.concatenate([from_r[64:68], blank, from_l[64:68]], axis=0))
    for ch in range(4):
        tail = jnp.where(at_right, turned[8 * ch : 8 * ch + 8], 0.0)
        tail = tail + jnp.where(at_left, turned[32 + 8 * ch : 40 + 8 * ch], 0.0)
        c3[ch, 136:144, COLS:] = tail

    largest = jnp.ones((8, WIDE), F32)
    for ch in range(4):
        for i in range(EXT // 8):
            largest = jnp.maximum(largest, jnp.abs(c3[ch, 8 + 8 * i : 16 + 8 * i, :]))
    scale = 1.0 / jnp.max(jnp.max(largest, axis=0, keepdims=True), axis=1, keepdims=True)
    w3[...] = w3[...] * (scale * scale)

    lane3 = iota((8, WIDE), 1)
    gx = jnp.where(lane3 >= WIDE - RIM, lane3 - WIDE, lane3) + region * COLS
    here_x = (gx >= 0) & (gx < REGIONS * COLS) & ((lane3 < COLS + RIM) | (lane3 >= WIDE - RIM))
    east_x = here_x & (gx >= 0) & (gx + 1 < REGIONS * COLS) & (lane3 != COLS + RIM - 1)
    st[:, 0:1, :] = jnp.zeros((5, 1, WIDE), F32)
    st[:, EXT + 1 : EXT + 2, :] = jnp.zeros((5, 1, WIDE), F32)
    for i in range(EXT // 8):
        at = 8 + 8 * i
        gy = tile * ROWS - RIM + 8 * i + iota((8, WIDE), 0)
        here_y = (gy >= 0) & (gy < TILES * ROWS)
        north_y = (gy >= 0) & (gy + 1 < TILES * ROWS)
        south_y = (gy >= 1) & (gy < TILES * ROWS)

        def near(ch, dy):
            x = c3[ch, at : at + 8, :]
            if dy == 1:
                x = jnp.concatenate([x[1:8], c3[ch, at + 8 : at + 16, :][0:1]], axis=0)
            if dy == -1:
                x = jnp.concatenate([c3[ch, at - 8 : at, :][7:8], x[0:7]], axis=0)
            return x

        h11, h22, mixed = near(0, 0), near(1, 0), near(2, 0)
        e, wst = 0.5 * (east(h11) + h11), 0.5 * (west(h11) + h11)
        n, s = 0.5 * (near(1, 1) + h22), 0.5 * (near(1, -1) + h22)
        rows = slice(8 * i + 1, 8 * i + 9)
        side = east(mixed)
        st[0, rows, :] = jnp.where(here_x & here_y, scale * (near(3, 0) + ((e + wst) + (n + s))), 0.0)
        st[1, rows, :] = jnp.where(east_x & here_y, -scale * e, 0.0)
        st[2, rows, :] = jnp.where(here_x & north_y, -scale * n, 0.0)
        st[3, rows, :] = jnp.where(east_x & north_y, (-0.25 * scale) * (side + near(2, 1)), 0.0)
        st[4, rows, :] = jnp.where(east_x & south_y, (0.25 * scale) * (side + near(2, -1)), 0.0)

    def apply(src, start, count, finish, put):
        def cells(r):
            x = src[r + 1]
            return x, east(x), [st[k, r + 1 : r + 2, :] for k in range(5)]

        below, here = cells(start - 1), cells(start)
        for r in range(start, start + count):
            above = cells(r + 1)
            (v0, e0, c0), (v1, e1, c1), (v2, e2, c2) = below, here, above
            from_west = c1[1] * v1 + c0[3] * v0 + c2[4] * v2
            total = c1[0] * v1 + c1[1] * e1 + c1[2] * v2 + c0[2] * v0
            total = total + (c1[3] * e2 + c1[4] * e0) + west(from_west)
            put(r, finish(r, total))
            below, here = here, above

    def plain(r, total):
        return total

    def with_b(r, total):
        return PREC_SCALE * total + w3[pl.ds(r, 1), :] * b3[r + 1]

    sums = [jnp.zeros((REALS, COLS), F32) for _ in range(3)]

    def with_q(r, total):
        q = q3[r + 1, :, 0:COLS]
        x = b3[r + 1, :, 0:COLS]
        t = PREC_SCALE * total[:, :COLS] + w3[pl.ds(r, 1), 0:COLS] * q
        sums[:] = [sums[0] + x * x, sums[1] + x * q, sums[2] + x * t]
        return q, t

    def put_f(r, x):
        f[r + 1] = x

    def put_q(r, x):
        q3[r + 1] = x

    def put_t(r, x):
        q_out[r - RIM] = x[0]
        t_out[r - RIM] = x[1]

    apply(b3, 0, EXT, plain, put_f)
    apply(f, 0, EXT, with_b, put_q)
    apply(q3, 0, EXT, plain, put_f)
    apply(f, RIM, ROWS, with_q, put_t)

    def total(x):
        return jnp.sum(x, axis=1, keepdims=True)

    bb, bq, bt = [total(x) for x in sums]
    safe = jnp.where(bb > 0.0, bb, 1.0)
    sigma, tau = bq / safe, bt / safe

    def second(i, acc):
        uu, uz = acc
        for d in range(8):
            r = 8 * i + d
            x = b[r + RIM]
            u = q_out[r] - sigma * x
            uu, uz = uu + u * u, uz + u * (t_out[r] - tau * x)
        return uu, uz

    zero = jnp.zeros((REALS, COLS), F32)
    uu, uz = [total(x) for x in lax.fori_loop(0, ROWS // 8, second, (zero, zero))]
    mu = uz / jnp.where(uu > 0.0, uu, 1.0)
    inverse = 1.0 / (scale * scale)
    own[...] = jnp.broadcast_to(inverse, (8, 128))
    column = [jnp.broadcast_to(x, (8, 128)) for x in (bb, sigma, uu, tau, mu, inverse)]
    moments[...] = jnp.transpose(jnp.concatenate(column + [jnp.zeros((80, 128), F32)], axis=0))


def finish_body(moments, own, b, q, t, x_out, r_out, x_own, r_own, leave):
    turned = jnp.transpose(moments[...])
    bb, sigma, uu, tau, mu, inverse = [turned[8 * m : 8 * m + 8] for m in range(6)]

    def total(x):
        return jnp.sum(x, axis=1, keepdims=True)

    norm0 = total(bb)
    alpha0 = norm0 / total(bb * sigma * inverse)
    a = alpha0 * inverse
    off = 1.0 - a * sigma
    norm1 = total(off * off * bb + a * a * uu)
    beta = norm1 / norm0
    grow = 1.0 + beta
    along = (grow - a * sigma) * (grow * sigma - a * tau) * bb
    curve = total(inverse * (along - a * (grow - a * mu) * uu))
    alpha1 = norm1 / curve
    mine = own[:, 0:1]
    a0 = alpha0 * mine
    a1 = alpha1 * mine

    copies = []
    for i in range(ROWS // PART):
        for r in range(PART * i, PART * i + PART):
            x, y, z = b[r + RIM], q[r], t[r]
            r1 = x - a0 * y
            d1 = r1 + beta * x
            x_own[r] = alpha0 * x + alpha1 * d1
            r_own[r] = r1 - a1 * (grow * y - a0 * z)
        rows = pl.ds(PART * i, PART)
        copies.append(pltpu.make_async_copy(x_own.at[rows], x_out.at[rows], leave.at[0, i]))
        copies.append(pltpu.make_async_copy(r_own.at[rows], r_out.at[rows], leave.at[1, i]))
        for c in copies[-2:]:
            c.start()
    for c in copies:
        c.wait()


def call(body, shapes, scratch, *args, ins=None, outs=None, limit=VMEM_LIMIT):
    ins = ins or [pltpu.VMEM] * len(args)
    outs = outs or [pltpu.VMEM] * len(shapes)
    return pl.pallas_call(
        body,
        out_shape=[jax.ShapeDtypeStruct(s, F32) for s in shapes],
        in_specs=[pl.BlockSpec(memory_space=m) for m in ins],
        out_specs=[pl.BlockSpec(memory_space=m) for m in outs],
        scratch_shapes=scratch,
        compiler_params=pltpu.CompilerParams(vmem_limit_bytes=limit),
    )(*args)


def local(coeffs, obs_cell, obs_value, obs_count):
    def ring(x, axis, size, step):
        return lax.ppermute(x, axis, [(i, (i + step) % size) for i in range(size)])

    south = ring(coeffs[:, ROWS - RIM :, :], "tile", TILES, 1)
    north = ring(coeffs[:, :RIM, :], "tile", TILES, -1)
    (packed,) = call(
        sort_body,
        [(TILES, 72, 128)],
        [
            pltpu.VMEM((1, SLOTS), I32),
            pltpu.VMEM((REALS, SLOTS), F32),
            pltpu.SemaphoreType.DMA((2,)),
        ],
        obs_count,
        obs_cell.reshape(1, SLOTS),
        obs_value,
        ins=[pltpu.SMEM, pltpu.HBM, pltpu.HBM],
        limit=60 * 1024 * 1024,
    )
    packed, south, north = lax.optimization_barrier((packed, south, north))
    recv = lax.all_to_all(packed, "tile", 0, 0)
    b, w, cp, edge_l, edge_r = call(
        scatter_body,
        [(EXT, REALS, COLS), (EXT, COLS), (4, EXT, COLS), (72, 128), (72, 128)],
        [
            pltpu.VMEM((REALS, DENSE), F32),
            pltpu.VMEM((REALS, DENSE), I32),
            pltpu.VMEM((COLS, DENSE), BF16),
            pltpu.VMEM((4, 16 * PIECE + 48, DENSE), BF16),
            pltpu.VMEM((4, 40, COLS), F32),
        ],
        recv,
        coeffs,
        south,
        north,
    )
    from_l = ring(edge_r, "region", REGIONS, 1)
    from_r = ring(edge_l, "region", REGIONS, -1)
    field = (ROWS, REALS, COLS)
    q, t, moments, own = call(
        krylov_body,
        [field, field, (128, 128), (8, 128)],
        [
            pltpu.VMEM((EXT + 2, REALS, WIDE), F32),
            pltpu.VMEM((EXT, WIDE), F32),
            pltpu.VMEM((4, EXT + 16, WIDE), F32),
            pltpu.VMEM((5, EXT + 2, WIDE), F32),
            pltpu.VMEM((EXT + 2, REALS, WIDE), F32),
            pltpu.VMEM((EXT + 2, REALS, WIDE), F32),
            pltpu.VMEM((72, 128), F32),
            pltpu.VMEM((72, 128), F32),
        ],
        b,
        w,
        cp,
        from_l,
        from_r,
    )
    shared = lax.all_to_all(moments, ("region", "tile"), 0, 0, tiled=True)
    return tuple(
        call(
            finish_body,
            [field, field],
            [
                pltpu.VMEM(field, F32),
                pltpu.VMEM(field, F32),
                pltpu.SemaphoreType.DMA((2, ROWS // PART)),
            ],
            shared,
            own,
            b,
            q,
            t,
            outs=[pltpu.HBM, pltpu.HBM],
        )
    )


def solution(mesh):
    placed = (
        P(None, "tile", "region"),
        P(("region", "tile")),
        P(None, ("region", "tile")),
        P(("region", "tile")),
    )
    return jax.shard_map(
        local,
        mesh=mesh,
        in_specs=placed,
        out_specs=(P("tile", None, "region"), P("tile", None, "region")),
        check_vma=False,
    )
```

time: 72.6 us -> 62.5 us (0.86)
  blocking collectives: 16.3 us -> 29.1 us
  starting transfers between devices: 21 us -> 10.8 us
  Pallas kernels: 22.1 us -> 14.3 us
  waiting for transfers between devices: 9.09 us -> 5.82 us
  local copies, waits for them, and re-layouts: 2.3 us -> 0.84 us
    all_to_all x0 -> x1, blocking collectives: none -> 14.3 us  [local(): recv = lax.all_to_all(packed, 'tile', 0, 0)]
    all_to_all x1 -> x0, starting transfers between devices: 8.43 us -> none  [local(): lax.all_to_all(jnp.broadcast_to(packed[None], (TILES, 72, 128)), 'tile',...]
    pallas_call x4, Pallas kernels: 22.1 us -> 14.3 us  [call(): pl.pallas_call(body, out_shape=[jax.ShapeDtypeStruct(s, F32) for s in sha...]
    all_to_all x1 -> x0, waiting for transfers between devices: 2.96 us -> none  [local(): lax.all_to_all(jnp.broadcast_to(packed[None], (TILES, 72, 128)), 'tile',...]
    ppermute x4, starting transfers between devices: 12.6 us -> 10.8 us  [ring(): return lax.ppermute(x, axis, [(i, (i + step) % size) for i in range(size)])]
    all_to_all x1, blocking collectives: 16.3 us -> 14.9 us  [local(): shared = lax.all_to_all(moments, ('region', 'tile'), 0, 0, tiled=True)]
    unnamed x6 -> x2, local copies, waits for them, and re-layouts: 1.44 us -> 0.01 us
    broadcast_in_dim x1 -> x0, local copies, waits for them, and re-layouts: 0.85 us -> none  [local(): jnp.broadcast_to(packed[None], (TILES, 72, 128))]
  transfers between devices with their start and end apart: 5 -> 4, of which waited for: 3 -> 3; matrix products, arithmetic and copies ran while one was open for 0% -> 0% of each run, Pallas kernels for 0% -> 5%
where the time goes in v2:
time: 62.5 us; the launch traced here: 62.2 us
  blocking collectives  29.1 us (47%)
  Pallas kernels  14.3 us (23%)
  starting transfers between devices  10.8 us (17%)
  waiting for transfers between devices  5.82 us (9%)
  between operations  1.32 us (2%)
  local copies, waits for them, and re-layouts  0.84 us (1%)
    all_to_all x1, blocking collectives, local(): shared = lax.all_to_all(moments, ('region', 'tile'), 0, 0, tiled=True)  14.9 us
    pallas_call x4, Pallas kernels, call(): pl.pallas_call(body, out_shape=[jax.ShapeDtypeStruct(s, F32) for s in sha...  14.3 us
    all_to_all x1, blocking collectives, local(): recv = lax.all_to_all(packed, 'tile', 0, 0)  14.3 us
    ppermute x4, starting transfers between devices, ring(): return lax.ppermute(x, axis, [(i, (i + step) % size) for i in range(size)])  10.8 us
    ppermute x4, waiting for transfers between devices, ring(): return lax.ppermute(x, axis, [(i, (i + step) % size) for i in range(size)])  5.82 us
  transfers between devices with their start and end apart: 4, of which 3 were waited for; matrix products, arithmetic and copies ran while one was open for 0% of the time, Pallas kernels for 5%

profile of v2, /device:TPU:1, one launch (start us, length us, event | category | flops | bytes accessed | tf_op | source)
XLA Modules:
  0.0 62.2 jit_solution(13929228247567441789)
XLA Ops:
  0.6 0.0 copy-start
  0.6 0.8 %fusion = (f32[4,4,256]{2,1,0:T(4,128)S(1)}, f32[4,4,256]{2,1,0:T(4,128)S(1)}) fusion(f32[4,128,256]{2,1,0:T(8,128)} %coef.1), kind=kLoop, calls=%fused_computation | loop fusion | bytes 65536 | tf_op jit(solution)/shard_map/slice | solution.py:400
  1.5 6.8 %collective-permute-start.1 = (f32[4,4,256]{2,1,0:T(4,128)S(1)}, f32[4,4,256]{2,1,0:T(4,128)S(1)}, u32[]{:S(2)}, u32[]{:S(2)}) collective-permute-start(f32[4,4,256]{2,1,0:T(4,128)S(1)} %get-tuple-element.26), channel_id=1, source_target_pairs={{0,15},{1,0},{2,1},{3,2},{4,3},{5,4},{6,5},{7,6},{8,7},{9,8},{10,9... | collective-permute-start | bytes 49160 | tf_op jit(solution)/shard_map/ppermute | solution.py:397
  8.3 0.0 collective-permute-start
  9.0 2.8 %shard_map.59 = f32[16,72,128]{2,1,0:T(8,128)} custom-call(s32[1]{0:T(128)S(6)} %copy.7.count, s32[1,1024]{1,0:T(1,128)} %bitcast.7, f32[8,1024]{1,0:T(8,128)} %value_hbm.1), custom_call_target="tpu_custom_call" | custom-call | tf_op jit(solution)/shard_map/pallas_call | solution.py:385
  11.8 0.0 collective-permute-done.1.north
  11.8 2.4 %collective-permute-done.south = f32[4,4,256]{2,1,0:T(4,128)S(1)} collective-permute-done((f32[4,4,256]{2,1,0:T(4,128)S(1)}, f32[4,4,256]{2,1,0:T(4,128)S(1)}, u32[]{:S(2)}, u32[]{:S(2)}) %collective-permute-start) | collective-permute-done | bytes 16416 | tf_op jit(solution)/shard_map/ppermute | solution.py:397
  14.2 14.3 %all_to_all.16.recv = f32[16,72,128]{2,1,0:T(8,128)S(1)} all-to-all(f32[16,72,128]{2,1,0:T(8,128)} %shard_map.59), channel_id=1, replica_groups=mesh['region'=8,'tile'=16] {'tile'}, dimensions={0} | all-to-all | bytes 1179648 | tf_op jit(solution)/shard_map/all_to_all | solution.py:416
  28.5 0.0 copy-done
  28.5 3.3 %shard_map.60 = (f32[136,8,256]{2,1,0:T(8,128)S(1)}, f32[136,256]{1,0:T(8,128)S(1)}, f32[4,136,256]{2,1,0:T(8,128)S(1)}, f32[72,128]{1,0:T(8,128)S(1)}, f32[72,128]{1,0:T(8,128)S(1)}) custom-call(f32[16,72,128]{2,1,0:T(8,128)S(1)} %all_to_all.16.recv, f32[4,128,256]{2,1,0:T(8,128)S(1)} %copy-done, f32[4,4,256]{2,1,0:T(4,128)S(1)} %collective-permute-done.south, ...), custom_call_target="tpu_custom_call" | custom-call | tf_op jit(solution)/shard_map/pallas_call | solution.py:385
  31.8 4.0 %collective-permute-start.2 = (f32[72,128]{1,0:T(8,128)S(1)}, f32[72,128]{1,0:T(8,128)S(1)}, u32[]{:S(2)}, u32[]{:S(2)}) collective-permute-start(f32[72,128]{1,0:T(8,128)S(1)} %get-tuple-element.20), channel_id=1, source_target_pairs={{0,16},{16,32},{32,48},{48,64},{64,80},{80,96},{96,112},{112,0},{1... | collective-permute-start | bytes 110600 | tf_op jit(solution)/shard_map/ppermute | solution.py:397
  35.7 0.0 collective-permute-start.3
  35.7 1.1 %collective-permute-done.2.got_l = f32[72,128]{1,0:T(8,128)S(1)} collective-permute-done((f32[72,128]{1,0:T(8,128)S(1)}, f32[72,128]{1,0:T(8,128)S(1)}, u32[]{:S(2)}, u32[]{:S(2)}) %collective-permute-start.2) | collective-permute-done | bytes 36896 | tf_op jit(solution)/shard_map/ppermute | solution.py:397
  36.8 2.3 %collective-permute-done.3.got_r = f32[72,128]{1,0:T(8,128)S(1)} collective-permute-done((f32[72,128]{1,0:T(8,128)S(1)}, f32[72,128]{1,0:T(8,128)S(1)}, u32[]{:S(2)}, u32[]{:S(2)}) %collective-permute-start.3) | collective-permute-done | bytes 36896 | tf_op jit(solution)/shard_map/ppermute | solution.py:397
  39.1 6.3 %shard_map.61 = (f32[128,8,256]{2,1,0:T(8,128)S(1)}, f32[128,8,256]{2,1,0:T(8,128)S(1)}, f32[128,128]{1,0:T(8,128)S(1)}, f32[8,128]{1,0:T(8,128)S(1)}) custom-call(f32[136,8,256]{2,1,0:T(8,128)S(1)} %get-tuple-element.17.b, f32[136,256]{1,0:T(8,128)S(1)} %get-tuple-element.18.w, f32[4,136,256]{2,1,0:T(8,128)S(1)} %get-tuple-element.19.cp, ...), custom_call_target="tpu_custom_call" | custom-call | tf_op jit(solution)/shard_map/pallas_call | solution.py:385
  45.5 14.9 %all_to_all.17 = f32[128,1,128]{2,1,0:T(1,128)S(1)} all-to-all(f32[128,1,128]{2,1,0:T(1,128)S(1)} %bitcast.6), channel_id=1, replica_groups=mesh['region'=8,'tile'=16] {'region','tile'}, dimensions={0} | all-to-all | bytes 131072 | tf_op jit(solution)/shard_map/all_to_all | solution.py:454
  60.3 1.9 %shard_map.62 = (f32[128,8,256]{2,1,0:T(8,128)}, f32[128,8,256]{2,1,0:T(8,128)}) custom-call(f32[128,128]{1,0:T(8,128)S(1)} %bitcast.5, f32[8,128]{1,0:T(8,128)S(1)} %get-tuple-element.23.own, f32[136,8,256]{2,1,0:T(8,128)S(1)} %get-tuple-element.17.b, f32[128,8,256]{2,1,0:T(8,128)S(1)} %get-tuple-element.24.q, f32[128,8,256]{2,1,0:T(8,128)S(1)} %get-tuple-element.25.t), custom_call_target="tpu_custom_call" | custom-call | tf_op jit(solution)/shard_map/pallas_call | solution.py:385
Async XLA Ops:
  0.6 27.9 %copy-start = (f32[4,128,256]{2,1,0:T(8,128)S(1)}, f32[4,128,256]{2,1,0:T(8,128)}, u32[]{:S(2)}) copy-start(f32[4,128,256]{2,1,0:T(8,128)} %coef.1) | copy-start | bytes 1572868
  1.5 10.3 %collective-permute-start.1 = (f32[4,4,256]{2,1,0:T(4,128)S(1)}, f32[4,4,256]{2,1,0:T(4,128)S(1)}, u32[]{:S(2)}, u32[]{:S(2)}) collective-permute-start(f32[4,4,256]{2,1,0:T(4,128)S(1)} %get-tuple-element.26), channel_id=1, source_target_pairs={{0,15},{1,0},{2,1},{3,2},{4,3},{5,4},{6,5},{7,6},{8,7},{9,8},{10,9... | collective-permute-start | bytes 49160 | tf_op jit(solution)/shard_map/ppermute | solution.py:397
  8.3 5.9 %collective-permute-start = (f32[4,4,256]{2,1,0:T(4,128)S(1)}, f32[4,4,256]{2,1,0:T(4,128)S(1)}, u32[]{:S(2)}, u32[]{:S(2)}) collective-permute-start(f32[4,4,256]{2,1,0:T(4,128)S(1)} %get-tuple-element.27), channel_id=1, source_target_pairs={{0,1},{1,2},{2,3},{3,4},{4,5},{5,6},{6,7},{7,8},{8,9},{9,10},{10,1... | collective-permute-start | bytes 49160 | tf_op jit(solution)/shard_map/ppermute | solution.py:397
  31.8 5.0 %collective-permute-start.2 = (f32[72,128]{1,0:T(8,128)S(1)}, f32[72,128]{1,0:T(8,128)S(1)}, u32[]{:S(2)}, u32[]{:S(2)}) collective-permute-start(f32[72,128]{1,0:T(8,128)S(1)} %get-tuple-element.20), channel_id=1, source_target_pairs={{0,16},{16,32},{32,48},{48,64},{64,80},{80,96},{96,112},{112,0},{1... | collective-permute-start | bytes 110600 | tf_op jit(solution)/shard_map/ppermute | solution.py:397
  35.7 3.4 %collective-permute-start.3 = (f32[72,128]{1,0:T(8,128)S(1)}, f32[72,128]{1,0:T(8,128)S(1)}, u32[]{:S(2)}, u32[]{:S(2)}) collective-permute-start(f32[72,128]{1,0:T(8,128)S(1)} %get-tuple-element.21), channel_id=1, source_target_pairs={{0,112},{16,0},{32,16},{48,32},{64,48},{80,64},{96,80},{112,96},{1... | collective-permute-start | bytes 110600 | tf_op jit(solution)/shard_map/ppermute | solution.py:397

commit v3 on v2

--- a/solution.py
+++ b/solution.py
@@ -12,6 +12,7 @@
 SLOTS = 1024
 TILES, REGIONS = 16, 8
 EXT = ROWS + 2 * RIM
+MESSAGE = 104
 WIDE = COLS + 128
 CHUNKS = SLOTS // 128
 SHARE = 96
@@ -31,10 +32,12 @@
     return lax.dot_general(a, b, (((1,), (1,)), ((), ())), preferred_element_type=F32)
 
 
-def sort_body(count, cell_hbm, value_hbm, out, cell_ref, value_ref, arrive):
+def sort_body(count, cell_hbm, value_hbm, coef_hbm, out, cell_ref, value_ref, low, high, arrive):
     copies = [
         pltpu.make_async_copy(cell_hbm, cell_ref, arrive.at[0]),
         pltpu.make_async_copy(value_hbm, value_ref, arrive.at[1]),
+        pltpu.make_async_copy(coef_hbm.at[:, pl.ds(0, 8), :], low, arrive.at[2]),
+        pltpu.make_async_copy(coef_hbm.at[:, pl.ds(ROWS - 8, 8), :], high, arrive.at[3]),
     ]
     for c in copies:
         c.start()
@@ -54,15 +57,14 @@
     code = jnp.where(live, cell, 4096 * 256)
     copies[1].wait()
     value = value_ref[...]
-    high = value.astype(BF16).astype(F32)
-    rest = value - high
+    top = value.astype(BF16).astype(F32)
+    rest = value - top
     middle = rest.astype(BF16).astype(F32)
-    low = rest - middle
     left = jnp.concatenate(
         [
-            high,
+            top,
             middle,
-            low,
+            rest - middle,
             (code & 255).astype(F32),
             ((code >> 8) & 255).astype(F32),
             (code >> 16).astype(F32),
@@ -80,16 +82,21 @@
             for s in range(TILES):
                 out[s, 8 * c : 8 * c + 8, :] = values[:, 128 * h : 128 * h + 128]
                 out[s, 64 + c : 65 + c, :] = codes[:, 128 * h : 128 * h + 128]
-
-
-def scatter_body(recv, coef, south, north, b, w, cp, edge_l, edge_r, vals, code, ct, a, hits):
+    copies[2].wait()
+    copies[3].wait()
+    tile = lax.axis_index("tile")
+    for ch in range(4):
+        x, y = low[ch, 0:RIM, :], high[ch, 8 - RIM : 8, :]
+        x = jnp.concatenate([x[:, 0:128], x[:, 128:256]], axis=0)
+        y = jnp.concatenate([y[:, 0:128], y[:, 128:256]], axis=0)
+        for s in range(TILES):
+            out[s, 72 + 8 * ch : 80 + 8 * ch, :] = jnp.where(tile + 1 == s, y, x)
+
+
+def scatter(recv, vals, code, one_round):
     first = lax.axis_index("tile") * ROWS - RIM
     low_cell = (first * COLS).astype(F32)
     high_cell = ((first + EXT) * COLS).astype(F32)
-    cp[:, RIM : RIM + ROWS, :] = coef[...]
-    tile = lax.axis_index("tile")
-    cp[:, :RIM, :] = jnp.where(tile == 0, 0.0, south[...])
-    cp[:, RIM + ROWS :, :] = jnp.where(tile == TILES - 1, 0.0, north[...])
     starts, lengths = [], []
     for s in range(TILES):
         cells = recv[s, 64:72, :]
@@ -100,11 +107,9 @@
     most = lengths[0]
     for x in lengths[1:]:
         most = jnp.maximum(most, x)
-    b[...] = jnp.zeros(b.shape, F32)
-    hits[...] = jnp.zeros(hits.shape, F32)
     lane = iota((1, 128), 1)
 
-    def one_round(k, carry):
+    def gather(k, carry):
         for chunk in range(DENSE // 128):
             value, local = jnp.zeros((REALS, 128), F32), jnp.full((8, 128), -COLS, I32)
             for s in range(128 * chunk // SHARE, (128 * chunk + 127) // SHARE + 1):
@@ -127,13 +132,65 @@
                 local = jnp.where(inside, cells, local)
             vals[:, 128 * chunk : 128 * chunk + 128] = value
             code[:, 128 * chunk : 128 * chunk + 128] = local
-        row = code[...] >> 8
-        column = code[0:1, :] & 255
         value = vals[...]
         high = value.astype(BF16).astype(F32)
-        low = value - high
+        one_round(code[...] >> 8, code[0:1, :] & 255, high, value - high)
+        return carry
+
+    lax.fori_loop(0, (most + SHARE - 1) // SHARE, gather, 0)
+
+
+def edge_body(recv, coef, cp, edge_l, edge_r, vals, code, ct, a, packed):
+    tile = lax.axis_index("tile")
+    cp[:, RIM : RIM + ROWS, :] = coef[...]
+    before, after = jnp.maximum(tile - 1, 0), jnp.minimum(tile + 1, TILES - 1)
+    for ch in range(4):
+        x = jnp.where(tile == 0, 0.0, recv[before, 72 + 8 * ch : 80 + 8 * ch, :])
+        y = jnp.where(tile == TILES - 1, 0.0, recv[after, 72 + 8 * ch : 80 + 8 * ch, :])
+        for h in range(2):
+            cp[ch, 0:RIM, 128 * h : 128 * h + 128] = x[RIM * h : RIM * h + RIM]
+            cp[ch, RIM + ROWS : EXT, 128 * h : 128 * h + 128] = y[RIM * h : RIM * h + RIM]
+    packed[...] = jnp.zeros(packed.shape, F32)
+
+    def one_round(row, column, high, low):
+        near = row[0:1]
+        spot = (near & 31) * 4 + column
+        spot = jnp.where(column >= COLS - RIM, spot + (128 - COLS + RIM), spot)
+        spot = jnp.where((column < RIM) | (column >= COLS - RIM), spot, -1)
+        ct[...] = jnp.where(iota((COLS, DENSE), 0) == spot, 1.0, 0.0).astype(BF16)
+        group = row >> 5
+        for g in range(GROUPS):
+            a[8 * g : 8 * g + 8, :] = jnp.where(group == g, high, 0.0).astype(BF16)
+            a[40 + 8 * g : 48 + 8 * g, :] = jnp.where(group == g, low, 0.0).astype(BF16)
+        ones = jnp.where(iota((16, DENSE), 0) == group[0:1], 1.0, 0.0)
+        a[80:96, :] = ones.astype(BF16)
+        got = contract_lanes(a[...], ct[...])
+        packed[0:40, :] += (got[0:40] + got[40:80]) * 2.0
+        packed[40:48, :] += got[80:88] * 2.0
+
+    scatter(recv, vals, code, one_round)
+
+    for side, edge in ((0, edge_l), (1, edge_r)):
+        cut = slice(0, 128) if side == 0 else slice(128, 256)
+        edge[0:48, :] = packed[:, cut]
+        keep = slice(0, RIM) if side == 0 else slice(128 - RIM, 128)
+        for ch in range(4):
+            turned = jnp.transpose(cp[ch, 0:128, cut])
+            edge[48 + 4 * ch : 52 + 4 * ch, :] = turned[keep]
+    tails = [cp[ch, 128:136, 128 * side : 128 * side + 128] for side in (0, 1) for ch in range(4)]
+    turned = jnp.transpose(jnp.concatenate(tails + [jnp.zeros((64, 128), F32)], axis=0))
+    edge_l[64:68, :] = turned[0:RIM]
+    edge_r[64:68, :] = turned[128 - RIM : 128]
+    edge_l[68:72, :] = jnp.zeros((4, 128), F32)
+    edge_r[68:72, :] = jnp.zeros((4, 128), F32)
+
+
+def scatter_body(recv, b, w, vals, code, ct, a, hits):
+    b[...] = jnp.zeros(b.shape, F32)
+    hits[...] = jnp.zeros(hits.shape, F32)
+
+    def one_round(row, column, high, low):
         ct[...] = jnp.where(iota((COLS, DENSE), 0) == column, 1.0, 0.0).astype(BF16)
-
         for p in range(4):
             base = p * PIECE
             for i in range(PIECE // 2):
@@ -149,40 +206,10 @@
             field = (got[: 8 * PIECE] + got[8 * PIECE : 16 * PIECE]) * 2.0
             b[base : base + PIECE] += field.reshape(PIECE, REALS, COLS)
             hits[p] += got[16 * PIECE : 16 * PIECE + 40] * 2.0
-        return carry
-
-    lax.fori_loop(0, (most + SHARE - 1) // SHARE, one_round, 0)
-
+
+    scatter(recv, vals, code, one_round)
     for p in range(4):
         w[PIECE * p : PIECE * p + PIECE, :] = hits[p, 0:PIECE]
-    lane8 = iota((8, 128), 1)
-    for side, edge in ((0, edge_l), (1, edge_r)):
-        cut = slice(0, 128) if side == 0 else slice(128, 256)
-        for g in range(GROUPS):
-            packed = jnp.zeros((8, 128), F32)
-            packed_w = jnp.zeros((1, 128), F32)
-            for j in range(min(32, EXT - 32 * g)):
-                r = 32 * g + j
-                turn = (4 * j + (0 if side == 0 else RIM)) % 128
-                mine = (lane8 >= 4 * j) & (lane8 < 4 * j + 4)
-                field, weight = b[r, :, cut], w[r : r + 1, cut]
-                if turn:
-                    field, weight = pltpu.roll(field, turn, 1), pltpu.roll(weight, turn, 1)
-                packed = jnp.where(mine, field, packed)
-                packed_w = jnp.where(mine[0:1], weight, packed_w)
-            edge[8 * g : 8 * g + 8, :] = packed
-            edge[40 + g : 41 + g, :] = packed_w
-        edge[45:48, :] = jnp.zeros((3, 128), F32)
-        keep = slice(0, RIM) if side == 0 else slice(128 - RIM, 128)
-        for ch in range(4):
-            turned = jnp.transpose(cp[ch, 0:128, cut])
-            edge[48 + 4 * ch : 52 + 4 * ch, :] = turned[keep]
-    tails = [cp[ch, 128:136, 128 * side : 128 * side + 128] for side in (0, 1) for ch in range(4)]
-    turned = jnp.transpose(jnp.concatenate(tails + [jnp.zeros((64, 128), F32)], axis=0))
-    edge_l[64:68, :] = turned[0:RIM]
-    edge_r[64:68, :] = turned[128 - RIM : 128]
-    edge_l[68:72, :] = jnp.zeros((4, 128), F32)
-    edge_r[68:72, :] = jnp.zeros((4, 128), F32)
 
 
 def krylov_body(b, w, cp, got_l, got_r, q_out, t_out, moments, own, b3, w3, c3, st, f, q3, from_l, from_r):
@@ -379,7 +406,7 @@
         c.wait()
 
 
-def call(body, shapes, scratch, *args, ins=None, outs=None, limit=VMEM_LIMIT):
+def call(body, shapes, scratch, *args, ins=None, outs=None, limit=VMEM_LIMIT, cost=None):
     ins = ins or [pltpu.VMEM] * len(args)
     outs = outs or [pltpu.VMEM] * len(shapes)
     return pl.pallas_call(
@@ -389,6 +416,7 @@
         out_specs=[pl.BlockSpec(memory_space=m) for m in outs],
         scratch_shapes=scratch,
         compiler_params=pltpu.CompilerParams(vmem_limit_bytes=limit),
+        cost_estimate=cost,
     )(*args)
 
 
@@ -396,27 +424,40 @@
     def ring(x, axis, size, step):
         return lax.ppermute(x, axis, [(i, (i + step) % size) for i in range(size)])
 
-    south = ring(coeffs[:, ROWS - RIM :, :], "tile", TILES, 1)
-    north = ring(coeffs[:, :RIM, :], "tile", TILES, -1)
     (packed,) = call(
         sort_body,
-        [(TILES, 72, 128)],
+        [(TILES, MESSAGE, 128)],
         [
             pltpu.VMEM((1, SLOTS), I32),
             pltpu.VMEM((REALS, SLOTS), F32),
-            pltpu.SemaphoreType.DMA((2,)),
+            pltpu.VMEM((4, 8, COLS), F32),
+            pltpu.VMEM((4, 8, COLS), F32),
+            pltpu.SemaphoreType.DMA((4,)),
         ],
         obs_count,
         obs_cell.reshape(1, SLOTS),
         obs_value,
-        ins=[pltpu.SMEM, pltpu.HBM, pltpu.HBM],
+        coeffs,
+        ins=[pltpu.SMEM, pltpu.HBM, pltpu.HBM, pltpu.HBM],
         limit=60 * 1024 * 1024,
     )
-    packed, south, north = lax.optimization_barrier((packed, south, north))
     recv = lax.all_to_all(packed, "tile", 0, 0)
-    b, w, cp, edge_l, edge_r = call(
+    cp, edge_l, edge_r = call(
+        edge_body,
+        [(4, EXT, COLS), (72, 128), (72, 128)],
+        [
+            pltpu.VMEM((REALS, DENSE), F32),
+            pltpu.VMEM((REALS, DENSE), I32),
+            pltpu.VMEM((COLS, DENSE), BF16),
+            pltpu.VMEM((96, DENSE), BF16),
+            pltpu.VMEM((48, COLS), F32),
+        ],
+        recv,
+        coeffs,
+    )
+    b, w = call(
         scatter_body,
-        [(EXT, REALS, COLS), (EXT, COLS), (4, EXT, COLS), (72, 128), (72, 128)],
+        [(EXT, REALS, COLS), (EXT, COLS)],
         [
             pltpu.VMEM((REALS, DENSE), F32),
             pltpu.VMEM((REALS, DENSE), I32),
@@ -425,9 +466,7 @@
             pltpu.VMEM((4, 40, COLS), F32),
         ],
         recv,
-        coeffs,
-        south,
-        north,
+        cost=pl.CostEstimate(flops=2 * 2368 * DENSE * COLS, bytes_accessed=1 << 23, transcendentals=0),
     )
     from_l = ring(edge_r, "region", REGIONS, 1)
     from_r = ring(edge_l, "region", REGIONS, -1)

time: 62.5 us -> 57.4 us (0.918)
  blocking collectives: 29.1 us -> 37.3 us
  starting transfers between devices: 10.8 us -> 3.03 us
  waiting for transfers between devices: 5.82 us -> 0.89 us
  local copies, waits for them, and re-layouts: 0.84 us -> 0.01 us
    all_to_all x1, blocking collectives: 14.3 us -> 22.7 us  [local(): recv = lax.all_to_all(packed, 'tile', 0, 0)]
    ppermute x4 -> x2, starting transfers between devices: 10.8 us -> 3.03 us  [ring(): return lax.ppermute(x, axis, [(i, (i + step) % size) for i in range(size)])]
    ppermute x4 -> x2, waiting for transfers between devices: 5.82 us -> 0.89 us  [ring(): return lax.ppermute(x, axis, [(i, (i + step) % size) for i in range(size)])]
    slice x1 -> x0, local copies, waits for them, and re-layouts: 0.84 us -> none  [local(): north = ring(coeffs[:, :RIM, :], 'tile', TILES, -1)]
    pallas_call x4 -> x5, Pallas kernels: 14.3 us -> 14.6 us  [call(): pl.pallas_call(body, out_shape=[jax.ShapeDtypeStruct(s, F32) for s in sha...]
  transfers between devices with their start and end apart: 4 -> 2, of which waited for: 3 -> 1; matrix products, arithmetic and copies ran while one was open for 0% -> 0% of each run, Pallas kernels for 5% -> 4%
where the time goes in v3:
time: 57.4 us; the launch traced here: 57.1 us
  blocking collectives  37.3 us (65%)
  Pallas kernels  14.6 us (25%)
  starting transfers between devices  3.03 us (5%)
  between operations  1.32 us (2%)
  waiting for transfers between devices  0.89 us (2%)
    all_to_all x1, blocking collectives, local(): recv = lax.all_to_all(packed, 'tile', 0, 0)  22.7 us
    pallas_call x5, Pallas kernels, call(): pl.pallas_call(body, out_shape=[jax.ShapeDtypeStruct(s, F32) for s in sha...  14.6 us
    all_to_all x1, blocking collectives, local(): shared = lax.all_to_all(moments, ('region', 'tile'), 0, 0, tiled=True)  14.5 us
    ppermute x2, starting transfers between devices, ring(): return lax.ppermute(x, axis, [(i, (i + step) % size) for i in range(size)])  3.03 us
  transfers between devices with their start and end apart: 2, of which 1 were waited for; matrix products, arithmetic and copies ran while one was open for 0% of the time, Pallas kernels for 4%

profile of v3, /device:TPU:1, one launch (start us, length us, event | category | flops | bytes accessed | tf_op | source)
XLA Modules:
  0.0 57.1 jit_solution(7458548358661455987)
XLA Ops:
  1.3 2.9 %shard_map.59 = f32[16,104,128]{2,1,0:T(8,128)} custom-call(s32[1]{0:T(128)S(6)} %copy.7.count, s32[1,1024]{1,0:T(1,128)} %bitcast.7, f32[8,1024]{1,0:T(8,128)} %value_hbm.1, f32[4,128,256]{2,1,0:T(8,128)} %coef.1), custom_call_target="tpu_custom_call" | custom-call | tf_op jit(solution)/shard_map/pallas_call | solution.py:412
  4.2 0.0 copy-start
  4.2 22.7 %all_to_all.16.recv = f32[16,104,128]{2,1,0:T(8,128)S(1)} all-to-all(f32[16,104,128]{2,1,0:T(8,128)} %shard_map.59), channel_id=1, replica_groups=mesh['region'=8,'tile'=16] {'tile'}, dimensions={0} | all-to-all | bytes 1703936 | tf_op jit(solution)/shard_map/all_to_all | solution.py:444
  27.0 0.0 copy-done
  27.0 1.0 %shard_map.61 = (f32[4,136,256]{2,1,0:T(8,128)S(1)}, f32[72,128]{1,0:T(8,128)S(1)}, f32[72,128]{1,0:T(8,128)S(1)}) custom-call(f32[16,104,128]{2,1,0:T(8,128)S(1)} %all_to_all.16.recv, f32[4,128,256]{2,1,0:T(8,128)S(1)} %copy-done), custom_call_target="tpu_custom_call" | custom-call | tf_op jit(solution)/shard_map/pallas_call | solution.py:412
  28.0 3.0 %collective-permute-start = (f32[72,128]{1,0:T(8,128)S(1)}, f32[72,128]{1,0:T(8,128)S(1)}, u32[]{:S(2)}, u32[]{:S(2)}) collective-permute-start(f32[72,128]{1,0:T(8,128)S(1)} %get-tuple-element.14), channel_id=1, source_target_pairs={{0,16},{16,32},{32,48},{48,64},{64,80},{80,96},{96,112},{112,0},{1... | collective-permute-start | bytes 110600 | tf_op jit(solution)/shard_map/ppermute | solution.py:425
  31.0 0.0 collective-permute-start.1
  31.0 2.5 %shard_map.60 = (f32[136,8,256]{2,1,0:T(8,128)S(1)}, f32[136,256]{1,0:T(8,128)S(1)}) custom-call(f32[16,104,128]{2,1,0:T(8,128)S(1)} %all_to_all.16.recv), custom_call_target="tpu_custom_call" | custom-call | flops 1862270976 | bytes 8388608 | tf_op jit(solution)/shard_map/pallas_call | solution.py:412
  33.5 0.0 collective-permute-done.got_l
  33.5 0.9 %collective-permute-done.1.got_r = f32[72,128]{1,0:T(8,128)S(1)} collective-permute-done((f32[72,128]{1,0:T(8,128)S(1)}, f32[72,128]{1,0:T(8,128)S(1)}, u32[]{:S(2)}, u32[]{:S(2)}) %collective-permute-start.1) | collective-permute-done | bytes 36896 | tf_op jit(solution)/shard_map/ppermute | solution.py:425
  34.4 6.3 %shard_map.62 = (f32[128,8,256]{2,1,0:T(8,128)S(1)}, f32[128,8,256]{2,1,0:T(8,128)S(1)}, f32[128,128]{1,0:T(8,128)S(1)}, f32[8,128]{1,0:T(8,128)S(1)}) custom-call(f32[136,8,256]{2,1,0:T(8,128)S(1)} %get-tuple-element.11.b, f32[136,256]{1,0:T(8,128)S(1)} %get-tuple-element.12.w, f32[4,136,256]{2,1,0:T(8,128)S(1)} %get-tuple-element.13.cp, ...), custom_call_target="tpu_custom_call" | custom-call | tf_op jit(solution)/shard_map/pallas_call | solution.py:412
  40.7 14.5 %all_to_all.17 = f32[128,1,128]{2,1,0:T(1,128)S(1)} all-to-all(f32[128,1,128]{2,1,0:T(1,128)S(1)} %bitcast.6), channel_id=1, replica_groups=mesh['region'=8,'tile'=16] {'region','tile'}, dimensions={0} | all-to-all | bytes 131072 | tf_op jit(solution)/shard_map/all_to_all | solution.py:493
  55.2 1.9 %shard_map.63 = (f32[128,8,256]{2,1,0:T(8,128)}, f32[128,8,256]{2,1,0:T(8,128)}) custom-call(f32[128,128]{1,0:T(8,128)S(1)} %bitcast.5, f32[8,128]{1,0:T(8,128)S(1)} %get-tuple-element.17.own, f32[136,8,256]{2,1,0:T(8,128)S(1)} %get-tuple-element.11.b, f32[128,8,256]{2,1,0:T(8,128)S(1)} %get-tuple-element.18.q, f32[128,8,256]{2,1,0:T(8,128)S(1)} %get-tuple-element.19.t), custom_call_target="tpu_custom_call" | custom-call | tf_op jit(solution)/shard_map/pallas_call | solution.py:412
Async XLA Ops:
  4.2 22.8 %copy-start = (f32[4,128,256]{2,1,0:T(8,128)S(1)}, f32[4,128,256]{2,1,0:T(8,128)}, u32[]{:S(2)}) copy-start(f32[4,128,256]{2,1,0:T(8,128)} %coef.1) | copy-start | bytes 1572868
  28.0 5.5 %collective-permute-start = (f32[72,128]{1,0:T(8,128)S(1)}, f32[72,128]{1,0:T(8,128)S(1)}, u32[]{:S(2)}, u32[]{:S(2)}) collective-permute-start(f32[72,128]{1,0:T(8,128)S(1)} %get-tuple-element.14), channel_id=1, source_target_pairs={{0,16},{16,32},{32,48},{48,64},{64,80},{80,96},{96,112},{112,0},{1... | collective-permute-start | bytes 110600 | tf_op jit(solution)/shard_map/ppermute | solution.py:425
  31.0 3.4 %collective-permute-start.1 = (f32[72,128]{1,0:T(8,128)S(1)}, f32[72,128]{1,0:T(8,128)S(1)}, u32[]{:S(2)}, u32[]{:S(2)}) collective-permute-start(f32[72,128]{1,0:T(8,128)S(1)} %get-tuple-element.15), channel_id=1, source_target_pairs={{0,112},{16,0},{32,16},{48,32},{64,48},{80,64},{96,80},{112,96},{1... | collective-permute-start | bytes 110600 | tf_op jit(solution)/shard_map/ppermute | solution.py:425

commit v4 on v3

--- a/solution.py
+++ b/solution.py
@@ -12,7 +12,9 @@
 SLOTS = 1024
 TILES, REGIONS = 16, 8
 EXT = ROWS + 2 * RIM
-MESSAGE = 104
+MESSAGE = 48
+LISTED = 72
+DEAD = 4096 * 256
 WIDE = COLS + 128
 CHUNKS = SLOTS // 128
 SHARE = 96
@@ -32,12 +34,11 @@
     return lax.dot_general(a, b, (((1,), (1,)), ((), ())), preferred_element_type=F32)
 
 
-def sort_body(count, cell_hbm, value_hbm, coef_hbm, out, cell_ref, value_ref, low, high, arrive):
+def sort_body(count, cell_hbm, value_hbm, coef_hbm, out, listed, cell_ref, value_ref, coef, arrive):
     copies = [
         pltpu.make_async_copy(cell_hbm, cell_ref, arrive.at[0]),
         pltpu.make_async_copy(value_hbm, value_ref, arrive.at[1]),
-        pltpu.make_async_copy(coef_hbm.at[:, pl.ds(0, 8), :], low, arrive.at[2]),
-        pltpu.make_async_copy(coef_hbm.at[:, pl.ds(ROWS - 8, 8), :], high, arrive.at[3]),
+        pltpu.make_async_copy(coef_hbm, coef, arrive.at[2]),
     ]
     for c in copies:
         c.start()
@@ -54,7 +55,7 @@
         for i in range(CHUNKS):
             below[i] = below[i] + jnp.where(column < across[i], 1.0, 0.0)
     rank = jnp.concatenate([jnp.sum(x, axis=0, keepdims=True) for x in below], axis=1).astype(I32)
-    code = jnp.where(live, cell, 4096 * 256)
+    code = jnp.where(live, cell, DEAD)
     copies[1].wait()
     value = value_ref[...]
     top = value.astype(BF16).astype(F32)
@@ -79,41 +80,106 @@
         codes = moved[24:25] + 256.0 * moved[25:26] + 65536.0 * moved[26:27]
         for h in range(2):
             c = 2 * k + h
-            for s in range(TILES):
-                out[s, 8 * c : 8 * c + 8, :] = values[:, 128 * h : 128 * h + 128]
-                out[s, 64 + c : 65 + c, :] = codes[:, 128 * h : 128 * h + 128]
-    copies[2].wait()
-    copies[3].wait()
-    tile = lax.axis_index("tile")
-    for ch in range(4):
-        x, y = low[ch, 0:RIM, :], high[ch, 8 - RIM : 8, :]
-        x = jnp.concatenate([x[:, 0:128], x[:, 128:256]], axis=0)
-        y = jnp.concatenate([y[:, 0:128], y[:, 128:256]], axis=0)
-        for s in range(TILES):
-            out[s, 72 + 8 * ch : 80 + 8 * ch, :] = jnp.where(tile + 1 == s, y, x)
-
-
-def scatter(recv, vals, code, one_round):
-    first = lax.axis_index("tile") * ROWS - RIM
-    low_cell = (first * COLS).astype(F32)
-    high_cell = ((first + EXT) * COLS).astype(F32)
+            listed[8 * c : 8 * c + 8, :] = values[:, 128 * h : 128 * h + 128]
+            listed[64 + c : 65 + c, :] = codes[:, 128 * h : 128 * h + 128]
+    cells = listed[64:72, :]
+    lane = iota((1, 128), 1)
     starts, lengths = [], []
     for s in range(TILES):
-        cells = recv[s, 64:72, :]
-        start = jnp.sum(jnp.where(cells < low_cell, 1.0, 0.0)).astype(I32)
-        end = jnp.sum(jnp.where(cells < high_cell, 1.0, 0.0)).astype(I32)
+        edge = [float((ROWS * s - RIM) * COLS), float((ROWS * s + ROWS + RIM) * COLS)]
+        start, end = [jnp.sum(jnp.where(cells < x, 1.0, 0.0)).astype(I32) for x in edge]
         starts.append(start)
         lengths.append(end - start)
     most = lengths[0]
     for x in lengths[1:]:
         most = jnp.maximum(most, x)
+    for s in range(TILES):
+        here = jnp.minimum(starts[s] >> 7, CHUNKS - 1)
+        after = jnp.minimum(here + 1, CHUNKS - 1)
+        at = starts[s] & 127
+        turn = (128 - at) & 127
+        head = lane < 128 - at
+        v0 = pltpu.roll(listed[pl.ds(pl.multiple_of(here * 8, 8), 8), :], turn, 1)
+        v1 = pltpu.roll(listed[pl.ds(pl.multiple_of(after * 8, 8), 8), :], turn, 1)
+        c0 = pltpu.roll(listed[pl.ds(64 + here, 1), :], turn, 1)
+        c1 = pltpu.roll(listed[pl.ds(64 + after, 1), :], turn, 1)
+        out[s, 0:8, :] = jnp.where(head, v0, v1)
+        out[s, 8:9, :] = jnp.where(lane < lengths[s], jnp.where(head, c0, c1), float(DEAD))
+        out[s, 9:10, :] = jnp.full((1, 128), most.astype(F32))
+        out[s, 10:11, :] = jnp.full((1, 128), lengths[s].astype(F32))
+        out[s, 11:16, :] = jnp.zeros((5, 128), F32)
+    copies[2].wait()
+    tile = lax.axis_index("tile")
+    for ch in range(4):
+        x, y = coef[ch, 0:RIM, :], coef[ch, ROWS - RIM : ROWS, :]
+        x = jnp.concatenate([x[:, 0:128], x[:, 128:256]], axis=0)
+        y = jnp.concatenate([y[:, 0:128], y[:, 128:256]], axis=0)
+        own = [
+            jnp.transpose(coef[ch, :, 0:128])[0:RIM],
+            jnp.transpose(coef[ch, :, 128:256])[128 - RIM : 128],
+        ]
+        own = jnp.concatenate(own, axis=0)
+        for s in range(TILES):
+            rows = jnp.where(tile == s, own, jnp.where(tile + 1 == s, y, x))
+            out[s, 16 + 8 * ch : 24 + 8 * ch, :] = rows
+
+
+def scatter(recv, whole, vals, code, one_round):
+    first = lax.axis_index("tile") * ROWS - RIM
     lane = iota((1, 128), 1)
-
-    def gather(k, carry):
+    most = recv[0, 10:11, :]
+    for s in range(1, TILES):
+        most = jnp.maximum(most, recv[s, 10:11, :])
+    most = jnp.max(most).astype(I32)
+
+    def put(chunk, value, cells):
+        vals[:, 128 * chunk : 128 * chunk + 128] = value
+        code[:, 128 * chunk : 128 * chunk + 128] = cells.astype(I32) - first * COLS
+
+    def blank():
+        return jnp.zeros((REALS, 128), F32), jnp.full((8, 128), float(DEAD), F32)
+
+    def head_of_block():
         for chunk in range(DENSE // 128):
-            value, local = jnp.zeros((REALS, 128), F32), jnp.full((8, 128), -COLS, I32)
+            value, cells = blank()
             for s in range(128 * chunk // SHARE, (128 * chunk + 127) // SHARE + 1):
-                begin = starts[s] + SHARE * k
+                offset = SHARE * s - 128 * chunk
+                x, y = recv[s, 0:8, :], jnp.broadcast_to(recv[s, 8:9, :], (8, 128))
+                if offset % 128:
+                    x, y = pltpu.roll(x, offset % 128, 1), pltpu.roll(y, offset % 128, 1)
+                inside = (lane >= offset) & (lane < offset + SHARE)
+                value, cells = jnp.where(inside, x, value), jnp.where(inside, y, cells)
+            put(chunk, value, cells)
+
+    def tail_of_block():
+        each = 128 - SHARE
+        per = 128 // each
+        for chunk in range(DENSE // 128):
+            value, cells = blank()
+            for s in range(per * chunk, min(per * chunk + per, TILES)):
+                offset = each * (s % per)
+                turn = (offset - SHARE) % 128
+                x = pltpu.roll(recv[s, 0:8, :], turn, 1)
+                y = pltpu.roll(jnp.broadcast_to(recv[s, 8:9, :], (8, 128)), turn, 1)
+                inside = (lane >= offset) & (lane < offset + each)
+                value, cells = jnp.where(inside, x, value), jnp.where(inside, y, cells)
+            put(chunk, value, cells)
+
+    def beyond_block(k):
+        low_cell = (first * COLS).astype(F32)
+        high_cell = ((first + EXT) * COLS).astype(F32)
+        starts, lengths = [], []
+        for s in range(TILES):
+            cells = whole[s, 64:72, :]
+            start = jnp.sum(jnp.where(cells < low_cell, 1.0, 0.0)).astype(I32)
+            end = jnp.sum(jnp.where(cells < high_cell, 1.0, 0.0)).astype(I32)
+            starts.append(start)
+            lengths.append(end - start)
+        done = 128 + SHARE * k
+        for chunk in range(DENSE // 128):
+            value, cells = blank()
+            for s in range(128 * chunk // SHARE, (128 * chunk + 127) // SHARE + 1):
+                begin = starts[s] + done
                 here = jnp.minimum(begin >> 7, CHUNKS - 1)
                 after = jnp.minimum(here + 1, CHUNKS - 1)
                 at = begin & 127
@@ -121,35 +187,38 @@
                 turn = (offset - at) & 127
                 spot = lane - offset
                 head = spot < 128 - at
-                inside = (spot >= 0) & (spot < SHARE) & (spot + SHARE * k < lengths[s])
-                v0 = pltpu.roll(recv[s, pl.ds(pl.multiple_of(here * 8, 8), 8), :], turn, 1)
-                v1 = pltpu.roll(recv[s, pl.ds(pl.multiple_of(after * 8, 8), 8), :], turn, 1)
-                c0 = jnp.broadcast_to(recv[s, pl.ds(64 + here, 1), :], (8, 128))
-                c1 = jnp.broadcast_to(recv[s, pl.ds(64 + after, 1), :], (8, 128))
+                inside = (spot >= 0) & (spot < SHARE) & (spot + done < lengths[s])
+                v0 = pltpu.roll(whole[s, pl.ds(pl.multiple_of(here * 8, 8), 8), :], turn, 1)
+                v1 = pltpu.roll(whole[s, pl.ds(pl.multiple_of(after * 8, 8), 8), :], turn, 1)
+                c0 = jnp.broadcast_to(whole[s, pl.ds(64 + here, 1), :], (8, 128))
+                c1 = jnp.broadcast_to(whole[s, pl.ds(64 + after, 1), :], (8, 128))
                 c0, c1 = pltpu.roll(c0, turn, 1), pltpu.roll(c1, turn, 1)
                 value = jnp.where(inside, jnp.where(head, v0, v1), value)
-                cells = jnp.where(head, c0, c1).astype(I32) - first * COLS
-                local = jnp.where(inside, cells, local)
-            vals[:, 128 * chunk : 128 * chunk + 128] = value
-            code[:, 128 * chunk : 128 * chunk + 128] = local
+                cells = jnp.where(inside, jnp.where(head, c0, c1), cells)
+            put(chunk, value, cells)
+
+    def step(k, carry):
+        pl.when(k == 0)(head_of_block)
+        pl.when(k == 1)(tail_of_block)
+        pl.when(k >= 2)(lambda: beyond_block(k - 2))
         value = vals[...]
         high = value.astype(BF16).astype(F32)
         one_round(code[...] >> 8, code[0:1, :] & 255, high, value - high)
         return carry
 
-    lax.fori_loop(0, (most + SHARE - 1) // SHARE, gather, 0)
-
-
-def edge_body(recv, coef, cp, edge_l, edge_r, vals, code, ct, a, packed):
+    extra = jnp.where(most > SHARE, 1, 0) + (jnp.maximum(most - 128, 0) + SHARE - 1) // SHARE
+    lax.fori_loop(0, 1 + extra, step, 0)
+
+
+def beside(recv, ch):
     tile = lax.axis_index("tile")
-    cp[:, RIM : RIM + ROWS, :] = coef[...]
     before, after = jnp.maximum(tile - 1, 0), jnp.minimum(tile + 1, TILES - 1)
-    for ch in range(4):
-        x = jnp.where(tile == 0, 0.0, recv[before, 72 + 8 * ch : 80 + 8 * ch, :])
-        y = jnp.where(tile == TILES - 1, 0.0, recv[after, 72 + 8 * ch : 80 + 8 * ch, :])
-        for h in range(2):
-            cp[ch, 0:RIM, 128 * h : 128 * h + 128] = x[RIM * h : RIM * h + RIM]
-            cp[ch, RIM + ROWS : EXT, 128 * h : 128 * h + 128] = y[RIM * h : RIM * h + RIM]
+    x = jnp.where(tile == 0, 0.0, recv[before, 16 + 8 * ch : 24 + 8 * ch, :])
+    y = jnp.where(tile == TILES - 1, 0.0, recv[after, 16 + 8 * ch : 24 + 8 * ch, :])
+    return x, y
+
+
+def edge_body(recv, whole, edge_l, edge_r, vals, code, ct, a, packed):
     packed[...] = jnp.zeros(packed.shape, F32)
 
     def one_round(row, column, high, low):
@@ -168,16 +237,15 @@
         packed[0:40, :] += (got[0:40] + got[40:80]) * 2.0
         packed[40:48, :] += got[80:88] * 2.0
 
-    scatter(recv, vals, code, one_round)
+    scatter(recv, whole, vals, code, one_round)
 
     for side, edge in ((0, edge_l), (1, edge_r)):
         cut = slice(0, 128) if side == 0 else slice(128, 256)
         edge[0:48, :] = packed[:, cut]
-        keep = slice(0, RIM) if side == 0 else slice(128 - RIM, 128)
         for ch in range(4):
-            turned = jnp.transpose(cp[ch, 0:128, cut])
-            edge[48 + 4 * ch : 52 + 4 * ch, :] = turned[keep]
-    tails = [cp[ch, 128:136, 128 * side : 128 * side + 128] for side in (0, 1) for ch in range(4)]
+            own = recv[lax.axis_index("tile"), 16 + 8 * ch : 24 + 8 * ch, :]
+            edge[48 + 4 * ch : 52 + 4 * ch, :] = own[RIM * side : RIM * side + RIM]
+    tails = [x[RIM * h : RIM * h + RIM] for h in (0, 1) for ch in range(4) for x in beside(recv, ch)]
     turned = jnp.transpose(jnp.concatenate(tails + [jnp.zeros((64, 128), F32)], axis=0))
     edge_l[64:68, :] = turned[0:RIM]
     edge_r[64:68, :] = turned[128 - RIM : 128]
@@ -185,7 +253,7 @@
     edge_r[68:72, :] = jnp.zeros((4, 128), F32)
 
 
-def scatter_body(recv, b, w, vals, code, ct, a, hits):
+def scatter_body(recv, whole, b, w, vals, code, ct, a, hits):
     b[...] = jnp.zeros(b.shape, F32)
     hits[...] = jnp.zeros(hits.shape, F32)
 
@@ -207,12 +275,12 @@
             b[base : base + PIECE] += field.reshape(PIECE, REALS, COLS)
             hits[p] += got[16 * PIECE : 16 * PIECE + 40] * 2.0
 
-    scatter(recv, vals, code, one_round)
+    scatter(recv, whole, vals, code, one_round)
     for p in range(4):
         w[PIECE * p : PIECE * p + PIECE, :] = hits[p, 0:PIECE]
 
 
-def krylov_body(b, w, cp, got_l, got_r, q_out, t_out, moments, own, b3, w3, c3, st, f, q3, from_l, from_r):
+def krylov_body(b, w, coef, recv, got_l, got_r, q_out, t_out, moments, own, b3, w3, c3, st, f, q3, from_l, from_r):
     region, tile = lax.axis_index("region"), lax.axis_index("tile")
     from_l[...] = jnp.where(region == 0, 0.0, got_l[...])
     from_r[...] = jnp.where(region == REGIONS - 1, 0.0, got_r[...])
@@ -248,16 +316,22 @@
         )
     c3[:, 0:8, :] = jnp.zeros((4, 8, WIDE), F32)
     c3[:, EXT + 8 :, :] = jnp.zeros((4, 8, WIDE), F32)
-    c3[:, 8 : EXT + 8, 0:COLS] = cp[...]
     blank = jnp.zeros((128 - 2 * RIM, 128), F32)
+    turned = jnp.transpose(jnp.concatenate([from_r[64:68], blank, from_l[64:68]], axis=0))
+    own_rows = slice(8 + RIM, 8 + RIM + ROWS)
     for ch in range(4):
+        c3[ch, own_rows, 0:COLS] = coef[ch]
+        south, north = beside(recv, ch)
+        for h in range(2):
+            half, cut = slice(RIM * h, RIM * h + RIM), slice(128 * h, 128 * h + 128)
+            c3[ch, 8 : 8 + RIM, cut] = south[half]
+            c3[ch, 8 + RIM + ROWS : 8 + EXT, cut] = north[half]
         s = slice(48 + 4 * ch, 52 + 4 * ch)
-        c3[ch, 8:136, COLS:] = jnp.transpose(jnp.concatenate([from_r[s], blank, from_l[s]], axis=0))
-    turned = jnp.transpose(jnp.concatenate([from_r[64:68], blank, from_l[64:68]], axis=0))
-    for ch in range(4):
+        c3[ch, own_rows, COLS:] = jnp.transpose(jnp.concatenate([from_r[s], blank, from_l[s]], axis=0))
         tail = jnp.where(at_right, turned[8 * ch : 8 * ch + 8], 0.0)
         tail = tail + jnp.where(at_left, turned[32 + 8 * ch : 40 + 8 * ch], 0.0)
-        c3[ch, 136:144, COLS:] = tail
+        c3[ch, 8 : 8 + RIM, COLS:] = tail[0:RIM]
+        c3[ch, 8 + RIM + ROWS : 8 + EXT, COLS:] = tail[RIM : 2 * RIM]
 
     largest = jnp.ones((8, WIDE), F32)
     for ch in range(4):
@@ -424,15 +498,14 @@
     def ring(x, axis, size, step):
         return lax.ppermute(x, axis, [(i, (i + step) % size) for i in range(size)])
 
-    (packed,) = call(
+    packed, listed = call(
         sort_body,
-        [(TILES, MESSAGE, 128)],
+        [(TILES, MESSAGE, 128), (LISTED, 128)],
         [
             pltpu.VMEM((1, SLOTS), I32),
             pltpu.VMEM((REALS, SLOTS), F32),
-            pltpu.VMEM((4, 8, COLS), F32),
-            pltpu.VMEM((4, 8, COLS), F32),
-            pltpu.SemaphoreType.DMA((4,)),
+            pltpu.VMEM((4, ROWS, COLS), F32),
+            pltpu.SemaphoreType.DMA((3,)),
         ],
         obs_count,
         obs_cell.reshape(1, SLOTS),
@@ -442,9 +515,17 @@
         limit=60 * 1024 * 1024,
     )
     recv = lax.all_to_all(packed, "tile", 0, 0)
-    cp, edge_l, edge_r = call(
+
+    def share(x):
+        return lax.all_to_all(jnp.broadcast_to(x[None], (TILES, LISTED, 128)), "tile", 0, 0)
+
+    def skip(x):
+        return jnp.zeros((TILES, LISTED, 128), F32)
+
+    whole = lax.cond(jnp.max(recv[:, 9, 0]) > 128.0, share, skip, listed)
+    edge_l, edge_r = call(
         edge_body,
-        [(4, EXT, COLS), (72, 128), (72, 128)],
+        [(72, 128), (72, 128)],
         [
             pltpu.VMEM((REALS, DENSE), F32),
             pltpu.VMEM((REALS, DENSE), I32),
@@ -453,7 +534,7 @@
             pltpu.VMEM((48, COLS), F32),
         ],
         recv,
-        coeffs,
+        whole,
     )
     b, w = call(
         scatter_body,
@@ -466,6 +547,7 @@
             pltpu.VMEM((4, 40, COLS), F32),
         ],
         recv,
+        whole,
         cost=pl.CostEstimate(flops=2 * 2368 * DENSE * COLS, bytes_accessed=1 << 23, transcendentals=0),
     )
     from_l = ring(edge_r, "region", REGIONS, 1)
@@ -486,7 +568,8 @@
         ],
         b,
         w,
-        cp,
+        coeffs,
+        recv,
         from_l,
         from_r,
     )

time: 57.4 us -> 53.6 us (0.934)
  blocking collectives: 37.3 us -> 14.6 us
  waiting for transfers between devices: 0.89 us -> 10.2 us
  starting transfers between devices: 3.03 us -> 11.5 us
  between operations: 1.32 us -> 1.98 us
  other arithmetic: 0 us -> 0.62 us
    all_to_all x1 -> x0, blocking collectives: 22.7 us -> none  [local(): recv = lax.all_to_all(packed, 'tile', 0, 0)]
    all_to_all x0 -> x1, waiting for transfers between devices: none -> 9.17 us  [local(): recv = lax.all_to_all(packed, 'tile', 0, 0)]
    all_to_all x0 -> x1, starting transfers between devices: none -> 8.44 us  [local(): recv = lax.all_to_all(packed, 'tile', 0, 0)]
    reduce_max x0 -> x1, other arithmetic: none -> 0.62 us  [local(): whole = lax.cond(jnp.max(recv[:, 9, 0]) > 128.0, share, skip, listed)]
  transfers between devices with their start and end apart: 2 -> 3, of which waited for: 1 -> 2; matrix products, arithmetic and copies ran while one was open for 0% -> 0% of each run, Pallas kernels for 4% -> 4%
where the time goes in v4:
time: 53.6 us; the launch traced here: 53.3 us
  blocking collectives  14.6 us (27%)
  Pallas kernels  14.3 us (27%)
  starting transfers between devices  11.5 us (21%)
  waiting for transfers between devices  10.2 us (19%)
  between operations  1.98 us (4%)
  other arithmetic  0.62 us (1%)
    all_to_all x1, blocking collectives, local(): shared = lax.all_to_all(moments, ('region', 'tile'), 0, 0, tiled=True)  14.6 us
    pallas_call x5, Pallas kernels, call(): pl.pallas_call(body, out_shape=[jax.ShapeDtypeStruct(s, F32) for s in sha...  14.3 us
    all_to_all x1, waiting for transfers between devices, local(): recv = lax.all_to_all(packed, 'tile', 0, 0)  9.17 us
    all_to_all x1, starting transfers between devices, local(): recv = lax.all_to_all(packed, 'tile', 0, 0)  8.44 us
    ppermute x2, starting transfers between devices, ring(): return lax.ppermute(x, axis, [(i, (i + step) % size) for i in range(size)])  3.08 us
  transfers between devices with their start and end apart: 3, of which 2 were waited for; matrix products, arithmetic and copies ran while one was open for 0% of the time, Pallas kernels for 4%

profile of v4, /device:TPU:1, one launch (start us, length us, event | category | flops | bytes accessed | tf_op | source)
XLA Modules:
  0.0 53.3 jit_solution(14377451007546475453)
XLA Ops:
  1.3 3.3 %shard_map.59 = (f32[16,48,128]{2,1,0:T(8,128)}, f32[72,128]{1,0:T(8,128)S(1)}) custom-call(s32[1]{0:T(128)S(6)} %copy.9.count, s32[1,1024]{1,0:T(1,128)} %bitcast.7, f32[8,1024]{1,0:T(8,128)} %value_hbm.1, f32[4,128,256]{2,1,0:T(8,128)} %coef.1), custom_call_target="tpu_custom_call" | custom-call | tf_op jit(solution)/shard_map/pallas_call | solution.py:486
  4.6 8.4 %all-to-all-start.1 = ((f32[16,48,128]{2,1,0:T(8,128)}), f32[16,48,128]{2,1,0:T(8,128)S(1)}, u32[]{:S(2)}, u32[]{:S(2)}) async-start(f32[16,48,128]{2,1,0:T(8,128)} %get-tuple-element.16), calls=%async_computation.1 | async-start | bytes 786432 | tf_op jit(solution)/shard_map/all_to_all | solution.py:517
  13.0 9.2 %all-to-all-done.1.recv = f32[16,48,128]{2,1,0:T(8,128)S(1)} async-done(((f32[16,48,128]{2,1,0:T(8,128)}), f32[16,48,128]{2,1,0:T(8,128)S(1)}, u32[]{:S(2)}, u32[]{:S(2)}) %all-to-all-start.1) | async-done | bytes 393248 | tf_op jit(solution)/shard_map/all_to_all | solution.py:517
  22.2 0.6 %slice_reduce_fusion = f32[]{:T(128)} fusion(f32[16,48,128]{2,1,0:T(8,128)S(1)} %all-to-all-done.1.recv), kind=kLoop, calls=%fused_computation | loop fusion | flops 15 | bytes 68 | tf_op jit(solution)/shard_map/reduce_max | solution.py:525
  23.4 0.1 conditional.1
  23.5 0.7 %shard_map.61 = (f32[72,128]{1,0:T(8,128)S(1)}, f32[72,128]{1,0:T(8,128)S(1)}) custom-call(f32[16,48,128]{2,1,0:T(8,128)S(1)} %all-to-all-done.1.recv, f32[16,72,128]{2,1,0:T(8,128)S(1)} %get-tuple-element.26.whole), custom_call_target="tpu_custom_call" | custom-call | tf_op jit(solution)/shard_map/pallas_call | solution.py:486
  24.3 3.1 %collective-permute-start = (f32[72,128]{1,0:T(8,128)S(1)}, f32[72,128]{1,0:T(8,128)S(1)}, u32[]{:S(2)}, u32[]{:S(2)}) collective-permute-start(f32[72,128]{1,0:T(8,128)S(1)} %get-tuple-element.20), channel_id=1, source_target_pairs={{0,16},{16,32},{32,48},{48,64},{64,80},{80,96},{96,112},{112,0},{1... | collective-permute-start | bytes 110600 | tf_op jit(solution)/shard_map/ppermute | solution.py:499
  27.3 0.0 copy-start
  27.3 0.0 collective-permute-start.1
  27.3 2.4 %shard_map.60 = (f32[136,8,256]{2,1,0:T(8,128)S(1)}, f32[136,256]{1,0:T(8,128)S(1)}) custom-call(f32[16,48,128]{2,1,0:T(8,128)S(1)} %all-to-all-done.1.recv, f32[16,72,128]{2,1,0:T(8,128)S(1)} %get-tuple-element.26.whole), custom_call_target="tpu_custom_call" | custom-call | flops 1862270976 | bytes 8388608 | tf_op jit(solution)/shard_map/pallas_call | solution.py:486
  29.7 0.0 collective-permute-done.got_l
  29.7 1.0 %collective-permute-done.1.got_r = f32[72,128]{1,0:T(8,128)S(1)} collective-permute-done((f32[72,128]{1,0:T(8,128)S(1)}, f32[72,128]{1,0:T(8,128)S(1)}, u32[]{:S(2)}, u32[]{:S(2)}) %collective-permute-start.1) | collective-permute-done | bytes 36896 | tf_op jit(solution)/shard_map/ppermute | solution.py:499
  30.7 0.0 copy-done
  30.7 6.1 %shard_map.62 = (f32[128,8,256]{2,1,0:T(8,128)S(1)}, f32[128,8,256]{2,1,0:T(8,128)S(1)}, f32[128,128]{1,0:T(8,128)S(1)}, f32[8,128]{1,0:T(8,128)S(1)}) custom-call(f32[136,8,256]{2,1,0:T(8,128)S(1)} %get-tuple-element.18.b, f32[136,256]{1,0:T(8,128)S(1)} %get-tuple-element.19.w, f32[4,128,256]{2,1,0:T(8,128)S(1)} %copy-done, ...), custom_call_target="tpu_custom_call" | custom-call | tf_op jit(solution)/shard_map/pallas_call | solution.py:486
  36.8 14.6 %all_to_all.21 = f32[128,1,128]{2,1,0:T(1,128)S(1)} all-to-all(f32[128,1,128]{2,1,0:T(1,128)S(1)} %bitcast.6), channel_id=1, replica_groups=mesh['region'=8,'tile'=16] {'region','tile'}, dimensions={0} | all-to-all | bytes 131072 | tf_op jit(solution)/shard_map/all_to_all | solution.py:576
  51.4 1.9 %shard_map.63 = (f32[128,8,256]{2,1,0:T(8,128)}, f32[128,8,256]{2,1,0:T(8,128)}) custom-call(f32[128,128]{1,0:T(8,128)S(1)} %bitcast.5, f32[8,128]{1,0:T(8,128)S(1)} %get-tuple-element.23.own, f32[136,8,256]{2,1,0:T(8,128)S(1)} %get-tuple-element.18.b, f32[128,8,256]{2,1,0:T(8,128)S(1)} %get-tuple-element.24.q, f32[128,8,256]{2,1,0:T(8,128)S(1)} %get-tuple-element.25.t), custom_call_target="tpu_custom_call" | custom-call | tf_op jit(solution)/shard_map/pallas_call | solution.py:486
  (1 shorter events, 0.0 us)
Async XLA Ops:
  4.6 17.6 %all-to-all-start.1 = ((f32[16,48,128]{2,1,0:T(8,128)}), f32[16,48,128]{2,1,0:T(8,128)S(1)}, u32[]{:S(2)}, u32[]{:S(2)}) async-start(f32[16,48,128]{2,1,0:T(8,128)} %get-tuple-element.16), calls=%async_computation.1 | async-start | bytes 786432 | tf_op jit(solution)/shard_map/all_to_all | solution.py:517
  24.3 5.5 %collective-permute-start = (f32[72,128]{1,0:T(8,128)S(1)}, f32[72,128]{1,0:T(8,128)S(1)}, u32[]{:S(2)}, u32[]{:S(2)}) collective-permute-start(f32[72,128]{1,0:T(8,128)S(1)} %get-tuple-element.20), channel_id=1, source_target_pairs={{0,16},{16,32},{32,48},{48,64},{64,80},{80,96},{96,112},{112,0},{1... | collective-permute-start | bytes 110600 | tf_op jit(solution)/shard_map/ppermute | solution.py:499
  27.3 3.4 %copy-start = (f32[4,128,256]{2,1,0:T(8,128)S(1)}, f32[4,128,256]{2,1,0:T(8,128)}, u32[]{:S(2)}) copy-start(f32[4,128,256]{2,1,0:T(8,128)} %coef.1) | copy-start | bytes 1572868
  27.3 3.4 %collective-permute-start.1 = (f32[72,128]{1,0:T(8,128)S(1)}, f32[72,128]{1,0:T(8,128)S(1)}, u32[]{:S(2)}, u32[]{:S(2)}) collective-permute-start(f32[72,128]{1,0:T(8,128)S(1)} %get-tuple-element.21), channel_id=1, source_target_pairs={{0,112},{16,0},{32,16},{48,32},{64,48},{80,64},{96,80},{112,96},{1... | collective-permute-start | bytes 110600 | tf_op jit(solution)/shard_map/ppermute | solution.py:499

commit v5 on v4

--- a/solution.py
+++ b/solution.py
@@ -12,8 +12,10 @@
 SLOTS = 1024
 TILES, REGIONS = 16, 8
 EXT = ROWS + 2 * RIM
-MESSAGE = 48
+MESSAGE = 40
 LISTED = 72
+PLACE = (32, 16, 24, 10)
+KEPT = (3, 4, 4, 3)
 DEAD = 4096 * 256
 WIDE = COLS + 128
 CHUNKS = SLOTS // 128
@@ -34,7 +36,7 @@
     return lax.dot_general(a, b, (((1,), (1,)), ((), ())), preferred_element_type=F32)
 
 
-def sort_body(count, cell_hbm, value_hbm, coef_hbm, out, listed, cell_ref, value_ref, coef, arrive):
+def sort_body(count, cell_hbm, value_hbm, coef_hbm, out, listed, space, cell_ref, value_ref, coef, arrive):
     copies = [
         pltpu.make_async_copy(cell_hbm, cell_ref, arrive.at[0]),
         pltpu.make_async_copy(value_hbm, value_ref, arrive.at[1]),
@@ -105,32 +107,30 @@
         c1 = pltpu.roll(listed[pl.ds(64 + after, 1), :], turn, 1)
         out[s, 0:8, :] = jnp.where(head, v0, v1)
         out[s, 8:9, :] = jnp.where(lane < lengths[s], jnp.where(head, c0, c1), float(DEAD))
-        out[s, 9:10, :] = jnp.full((1, 128), most.astype(F32))
-        out[s, 10:11, :] = jnp.full((1, 128), lengths[s].astype(F32))
-        out[s, 11:16, :] = jnp.zeros((5, 128), F32)
+        counts = jnp.where(lane < 64, most.astype(F32), lengths[s].astype(F32))
+        out[s, 9:10, :] = counts
+        out[s, 38:40, :] = jnp.zeros((2, 128), F32)
     copies[2].wait()
     tile = lax.axis_index("tile")
     for ch in range(4):
-        x, y = coef[ch, 0:RIM, :], coef[ch, ROWS - RIM : ROWS, :]
+        n = KEPT[ch]
+        x, y = coef[ch, 0:n, :], coef[ch, ROWS - n : ROWS, :]
         x = jnp.concatenate([x[:, 0:128], x[:, 128:256]], axis=0)
         y = jnp.concatenate([y[:, 0:128], y[:, 128:256]], axis=0)
-        own = [
-            jnp.transpose(coef[ch, :, 0:128])[0:RIM],
-            jnp.transpose(coef[ch, :, 128:256])[128 - RIM : 128],
-        ]
-        own = jnp.concatenate(own, axis=0)
         for s in range(TILES):
-            rows = jnp.where(tile == s, own, jnp.where(tile + 1 == s, y, x))
-            out[s, 16 + 8 * ch : 24 + 8 * ch, :] = rows
-
-
-def scatter(recv, whole, vals, code, one_round):
+            out[s, PLACE[ch] : PLACE[ch] + 2 * n, :] = jnp.where(tile + 1 == s, y, x)
+        at = LISTED + 8 * ch
+        listed[at : at + RIM, :] = jnp.transpose(coef[ch, :, 0:128])[0:RIM]
+        listed[at + RIM : at + 8, :] = jnp.transpose(coef[ch, :, 128:256])[128 - RIM : 128]
+
+
+def scatter(recv, whole, vals, code, one_round, block=True, beyond=True, fetch=None):
     first = lax.axis_index("tile") * ROWS - RIM
     lane = iota((1, 128), 1)
-    most = recv[0, 10:11, :]
+    most = recv[0, 9:10, :]
     for s in range(1, TILES):
-        most = jnp.maximum(most, recv[s, 10:11, :])
-    most = jnp.max(most).astype(I32)
+        most = jnp.maximum(most, recv[s, 9:10, :])
+    most = jnp.max(jnp.where(lane < 64, 0.0, most)).astype(I32)
 
     def put(chunk, value, cells):
         vals[:, 128 * chunk : 128 * chunk + 128] = value
@@ -197,30 +197,45 @@
                 cells = jnp.where(inside, jnp.where(head, c0, c1), cells)
             put(chunk, value, cells)
 
-    def step(k, carry):
-        pl.when(k == 0)(head_of_block)
-        pl.when(k == 1)(tail_of_block)
-        pl.when(k >= 2)(lambda: beyond_block(k - 2))
+    def finish_round():
         value = vals[...]
         high = value.astype(BF16).astype(F32)
         one_round(code[...] >> 8, code[0:1, :] & 255, high, value - high)
+
+    def block_round(k, carry):
+        pl.when(k == 0)(head_of_block)
+        pl.when(k == 1)(tail_of_block)
+        finish_round()
         return carry
 
-    extra = jnp.where(most > SHARE, 1, 0) + (jnp.maximum(most - 128, 0) + SHARE - 1) // SHARE
-    lax.fori_loop(0, 1 + extra, step, 0)
+    def beyond_round(k, carry):
+        beyond_block(k)
+        finish_round()
+        return carry
+
+    if block:
+        lax.fori_loop(0, jnp.where(most > SHARE, 2, 1), block_round, 0)
+    if beyond:
+        if fetch is not None:
+            pl.when(most > 128)(fetch)
+        lax.fori_loop(0, (jnp.maximum(most - 128, 0) + SHARE - 1) // SHARE, beyond_round, 0)
 
 
 def beside(recv, ch):
     tile = lax.axis_index("tile")
     before, after = jnp.maximum(tile - 1, 0), jnp.minimum(tile + 1, TILES - 1)
-    x = jnp.where(tile == 0, 0.0, recv[before, 16 + 8 * ch : 24 + 8 * ch, :])
-    y = jnp.where(tile == TILES - 1, 0.0, recv[after, 16 + 8 * ch : 24 + 8 * ch, :])
-    return x, y
-
-
-def edge_body(recv, whole, edge_l, edge_r, vals, code, ct, a, packed):
-    packed[...] = jnp.zeros(packed.shape, F32)
-
+    n = KEPT[ch]
+    rows = slice(PLACE[ch], PLACE[ch] + 2 * n)
+    x = jnp.where(tile == 0, 0.0, recv[before, rows, :])
+    y = jnp.where(tile == TILES - 1, 0.0, recv[after, rows, :])
+    if n == RIM:
+        return x, y
+    none = jnp.zeros((RIM - n, 128), F32)
+    x = jnp.concatenate([none, x[0:n], none, x[n:]], axis=0)
+    return x, jnp.concatenate([y[0:n], none, y[n:], none], axis=0)
+
+
+def edge_round(ct, a, packed):
     def one_round(row, column, high, low):
         near = row[0:1]
         spot = (near & 31) * 4 + column
@@ -237,23 +252,38 @@
         packed[0:40, :] += (got[0:40] + got[40:80]) * 2.0
         packed[40:48, :] += got[80:88] * 2.0
 
-    scatter(recv, whole, vals, code, one_round)
-
-    for side, edge in ((0, edge_l), (1, edge_r)):
-        cut = slice(0, 128) if side == 0 else slice(128, 256)
-        edge[0:48, :] = packed[:, cut]
-        for ch in range(4):
-            own = recv[lax.axis_index("tile"), 16 + 8 * ch : 24 + 8 * ch, :]
-            edge[48 + 4 * ch : 52 + 4 * ch, :] = own[RIM * side : RIM * side + RIM]
+    return one_round
+
+
+def edge_body(recv, listed, edge_l, edge_r, flag, vals, code, ct, a, packed):
+    most = recv[0, 9:10, :]
+    for s in range(1, TILES):
+        most = jnp.maximum(most, recv[s, 9:10, :])
+    flag[0] = jnp.where(jnp.max(most) > 128.0, 1, 0)
+    packed[...] = jnp.zeros(packed.shape, F32)
+    scatter(recv, None, vals, code, edge_round(ct, a, packed), beyond=False)
     tails = [x[RIM * h : RIM * h + RIM] for h in (0, 1) for ch in range(4) for x in beside(recv, ch)]
     turned = jnp.transpose(jnp.concatenate(tails + [jnp.zeros((64, 128), F32)], axis=0))
-    edge_l[64:68, :] = turned[0:RIM]
-    edge_r[64:68, :] = turned[128 - RIM : 128]
-    edge_l[68:72, :] = jnp.zeros((4, 128), F32)
-    edge_r[68:72, :] = jnp.zeros((4, 128), F32)
-
-
-def scatter_body(recv, whole, b, w, vals, code, ct, a, hits):
+    for side, edge in ((0, edge_l), (1, edge_r)):
+        edge[0:48, :] = packed[:, 128 * side : 128 * side + 128]
+        for ch in range(4):
+            at = LISTED + 8 * ch + RIM * side
+            edge[48 + 4 * ch : 52 + 4 * ch, :] = listed[at : at + RIM, :]
+        edge[64:68, :] = turned[(128 - RIM) * side : (128 - RIM) * side + RIM]
+        edge[68:72, :] = jnp.zeros((4, 128), F32)
+
+
+def rest_body(recv, whole, old_l, old_r, edge_l, edge_r, vals, code, ct, a, packed):
+    packed[:, 0:128] = old_l[0:48, :]
+    packed[:, 128:256] = old_r[0:48, :]
+    scatter(recv, whole, vals, code, edge_round(ct, a, packed), block=False)
+    edge_l[...] = old_l[...]
+    edge_r[...] = old_r[...]
+    edge_l[0:48, :] = packed[:, 0:128]
+    edge_r[0:48, :] = packed[:, 128:256]
+
+
+def scatter_body(recv, lists, b, w, vals, code, ct, a, hits, whole, arrive):
     b[...] = jnp.zeros(b.shape, F32)
     hits[...] = jnp.zeros(hits.shape, F32)
 
@@ -275,7 +305,12 @@
             b[base : base + PIECE] += field.reshape(PIECE, REALS, COLS)
             hits[p] += got[16 * PIECE : 16 * PIECE + 40] * 2.0
 
-    scatter(recv, whole, vals, code, one_round)
+    def fetch():
+        copy = pltpu.make_async_copy(lists, whole, arrive)
+        copy.start()
+        copy.wait()
+
+    scatter(recv, whole, vals, code, one_round, fetch=fetch)
     for p in range(4):
         w[PIECE * p : PIECE * p + PIECE, :] = hits[p, 0:PIECE]
 
@@ -412,9 +447,9 @@
         q_out[r - RIM] = x[0]
         t_out[r - RIM] = x[1]
 
-    apply(b3, 0, EXT, plain, put_f)
-    apply(f, 0, EXT, with_b, put_q)
-    apply(q3, 0, EXT, plain, put_f)
+    apply(b3, 1, EXT - 2, plain, put_f)
+    apply(f, 2, EXT - 4, with_b, put_q)
+    apply(q3, 3, EXT - 6, plain, put_f)
     apply(f, RIM, ROWS, with_q, put_t)
 
     def total(x):
@@ -480,12 +515,14 @@
         c.wait()
 
 
-def call(body, shapes, scratch, *args, ins=None, outs=None, limit=VMEM_LIMIT, cost=None):
+def call(body, shapes, scratch, *args, ins=None, outs=None, limit=VMEM_LIMIT, cost=None, types=None):
     ins = ins or [pltpu.VMEM] * len(args)
     outs = outs or [pltpu.VMEM] * len(shapes)
     return pl.pallas_call(
         body,
-        out_shape=[jax.ShapeDtypeStruct(s, F32) for s in shapes],
+        out_shape=[
+            jax.ShapeDtypeStruct(s, t) for s, t in zip(shapes, types or [F32] * len(shapes))
+        ],
         in_specs=[pl.BlockSpec(memory_space=m) for m in ins],
         out_specs=[pl.BlockSpec(memory_space=m) for m in outs],
         scratch_shapes=scratch,
@@ -498,9 +535,9 @@
     def ring(x, axis, size, step):
         return lax.ppermute(x, axis, [(i, (i + step) % size) for i in range(size)])
 
-    packed, listed = call(
+    packed, listed, space = call(
         sort_body,
-        [(TILES, MESSAGE, 128), (LISTED, 128)],
+        [(TILES, MESSAGE, 128), (LISTED + 32, 128), (TILES, LISTED, 128)],
         [
             pltpu.VMEM((1, SLOTS), I32),
             pltpu.VMEM((REALS, SLOTS), F32),
@@ -512,30 +549,38 @@
         obs_value,
         coeffs,
         ins=[pltpu.SMEM, pltpu.HBM, pltpu.HBM, pltpu.HBM],
+        outs=[pltpu.VMEM, pltpu.VMEM, pltpu.HBM],
         limit=60 * 1024 * 1024,
     )
     recv = lax.all_to_all(packed, "tile", 0, 0)
 
-    def share(x):
-        return lax.all_to_all(jnp.broadcast_to(x[None], (TILES, LISTED, 128)), "tile", 0, 0)
-
-    def skip(x):
-        return jnp.zeros((TILES, LISTED, 128), F32)
-
-    whole = lax.cond(jnp.max(recv[:, 9, 0]) > 128.0, share, skip, listed)
-    edge_l, edge_r = call(
+    work = [
+        pltpu.VMEM((REALS, DENSE), F32),
+        pltpu.VMEM((REALS, DENSE), I32),
+        pltpu.VMEM((COLS, DENSE), BF16),
+        pltpu.VMEM((96, DENSE), BF16),
+        pltpu.VMEM((48, COLS), F32),
+    ]
+    sides = [(72, 128), (72, 128)]
+    edge_l, edge_r, flag = call(
         edge_body,
-        [(72, 128), (72, 128)],
-        [
-            pltpu.VMEM((REALS, DENSE), F32),
-            pltpu.VMEM((REALS, DENSE), I32),
-            pltpu.VMEM((COLS, DENSE), BF16),
-            pltpu.VMEM((96, DENSE), BF16),
-            pltpu.VMEM((48, COLS), F32),
-        ],
+        sides + [(1,)],
+        work,
         recv,
-        whole,
+        listed,
+        outs=[pltpu.VMEM, pltpu.VMEM, pltpu.SMEM],
+        types=[F32, F32, I32],
     )
+
+    def share(recv, listed, space, edge_l, edge_r):
+        whole = jnp.broadcast_to(listed[None, :LISTED], (TILES, LISTED, 128))
+        whole = lax.all_to_all(whole, "tile", 0, 0)
+        return (whole, *call(rest_body, sides, work, recv, whole, edge_l, edge_r))
+
+    def skip(recv, listed, space, edge_l, edge_r):
+        return space, edge_l, edge_r
+
+    whole, edge_l, edge_r = lax.cond(flag[0] > 0, share, skip, recv, listed, space, edge_l, edge_r)
     b, w = call(
         scatter_body,
         [(EXT, REALS, COLS), (EXT, COLS)],
@@ -545,9 +590,12 @@
             pltpu.VMEM((COLS, DENSE), BF16),
             pltpu.VMEM((4, 16 * PIECE + 48, DENSE), BF16),
             pltpu.VMEM((4, 40, COLS), F32),
+            pltpu.VMEM((TILES, LISTED, 128), F32),
+            pltpu.SemaphoreType.DMA,
         ],
         recv,
         whole,
+        ins=[pltpu.VMEM, pltpu.HBM],
         cost=pl.CostEstimate(flops=2 * 2368 * DENSE * COLS, bytes_accessed=1 << 23, transcendentals=0),
     )
     from_l = ring(edge_r, "region", REGIONS, 1)

time: 53.6 us -> 52.5 us (0.979)
  blocking collectives: 14.6 us -> 31.5 us
  waiting for transfers between devices: 10.2 us -> 0.77 us
  starting transfers between devices: 11.5 us -> 3.06 us
  other arithmetic: 0.62 us -> 0 us
    all_to_all x0 -> x1, blocking collectives: none -> 16.9 us  [local(): recv = lax.all_to_all(packed, 'tile', 0, 0)]
    all_to_all x1 -> x0, waiting for transfers between devices: 9.17 us -> none  [local(): recv = lax.all_to_all(packed, 'tile', 0, 0)]
    all_to_all x1 -> x0, starting transfers between devices: 8.44 us -> none  [local(): recv = lax.all_to_all(packed, 'tile', 0, 0)]
    reduce_max x1 -> x0, other arithmetic: 0.62 us -> none  [local(): whole = lax.cond(jnp.max(recv[:, 9, 0]) > 128.0, share, skip, listed)]
  transfers between devices with their start and end apart: 3 -> 2, of which waited for: 2 -> 1; matrix products, arithmetic and copies ran while one was open for 0% -> 0% of each run, Pallas kernels for 4% -> 5%
where the time goes in v5:
time: 52.5 us; the launch traced here: 52.3 us
  blocking collectives  31.5 us (60%)
  Pallas kernels  14.8 us (28%)
  starting transfers between devices  3.06 us (6%)
  between operations  2.13 us (4%)
  waiting for transfers between devices  0.77 us (1%)
    all_to_all x1, blocking collectives, local(): recv = lax.all_to_all(packed, 'tile', 0, 0)  16.9 us
    pallas_call x5, Pallas kernels, call(): pl.pallas_call(body, out_shape=[jax.ShapeDtypeStruct(s, t) for s, t in zi...  14.8 us
    all_to_all x1, blocking collectives, local(): shared = lax.all_to_all(moments, ('region', 'tile'), 0, 0, tiled=True)  14.6 us
    ppermute x2, starting transfers between devices, ring(): return lax.ppermute(x, axis, [(i, (i + step) % size) for i in range(size)])  3.06 us
  transfers between devices with their start and end apart: 2, of which 1 were waited for; matrix products, arithmetic and copies ran while one was open for 0% of the time, Pallas kernels for 5%

profile of v5, /device:TPU:1, one launch (start us, length us, event | category | flops | bytes accessed | tf_op | source)
XLA Modules:
  0.0 52.3 jit_solution(6625210307079423397)
XLA Ops:
  1.3 3.2 %shard_map.59 = (f32[16,40,128]{2,1,0:T(8,128)}, f32[104,128]{1,0:T(8,128)S(1)}, f32[16,72,128]{2,1,0:T(8,128)}) custom-call(s32[1]{0:T(128)S(6)} %copy.15.count, s32[1,1024]{1,0:T(1,128)} %bitcast.8, f32[8,1024]{1,0:T(8,128)} %value_hbm.1, f32[4,128,256]{2,1,0:T(8,128)} %coef.1), custom_call_target="tpu_custom_call" | custom-call | tf_op jit(solution)/shard_map/pallas_call | solution.py:521
  4.5 16.9 %all_to_all.20.recv = f32[16,40,128]{2,1,0:T(8,128)S(1)} all-to-all(f32[16,40,128]{2,1,0:T(8,128)} %get-tuple-element.37), channel_id=1, replica_groups=mesh['region'=8,'tile'=16] {'tile'}, dimensions={0} | all-to-all | bytes 655360 | tf_op jit(solution)/shard_map/all_to_all | solution.py:555
  21.4 0.8 %shard_map.60 = (f32[72,128]{1,0:T(8,128)S(1)}, f32[72,128]{1,0:T(8,128)S(1)}, s32[1]{0:T(128)}) custom-call(f32[16,40,128]{2,1,0:T(8,128)S(1)} %all_to_all.20.recv, f32[104,128]{1,0:T(8,128)S(1)} %get-tuple-element.38.listed), custom_call_target="tpu_custom_call" | custom-call | tf_op jit(solution)/shard_map/pallas_call | solution.py:521
  22.8 3.1 %collective-permute-start = (f32[72,128]{1,0:T(8,128)S(1)}, f32[72,128]{1,0:T(8,128)S(1)}, u32[]{:S(2)}, u32[]{:S(2)}) collective-permute-start(f32[72,128]{1,0:T(8,128)S(1)} %get-tuple-element.46), channel_id=1, source_target_pairs={{0,16},{16,32},{32,48},{48,64},{64,80},{80,96},{96,112},{112,0},{1... | collective-permute-start | bytes 110600 | tf_op jit(solution)/shard_map/ppermute | solution.py:536
  25.9 0.0 collective-permute-start.1
  25.9 0.0 copy-start
  25.9 2.6 %shard_map.61 = (f32[136,8,256]{2,1,0:T(8,128)S(1)}, f32[136,256]{1,0:T(8,128)S(1)}) custom-call(f32[16,40,128]{2,1,0:T(8,128)S(1)} %all_to_all.20.recv, f32[16,72,128]{2,1,0:T(8,128)} %get-tuple-element.43.lists), custom_call_target="tpu_custom_call" | custom-call | flops 1862270976 | bytes 8388608 | tf_op jit(solution)/shard_map/pallas_call | solution.py:521
  28.5 0.0 collective-permute-done.got_l
  28.5 0.8 %collective-permute-done.1.got_r = f32[72,128]{1,0:T(8,128)S(1)} collective-permute-done((f32[72,128]{1,0:T(8,128)S(1)}, f32[72,128]{1,0:T(8,128)S(1)}, u32[]{:S(2)}, u32[]{:S(2)}) %collective-permute-start.1) | collective-permute-done | bytes 36896 | tf_op jit(solution)/shard_map/ppermute | solution.py:536
  29.3 0.0 copy-done
  29.3 6.3 %shard_map.62 = (f32[128,8,256]{2,1,0:T(8,128)S(1)}, f32[128,8,256]{2,1,0:T(8,128)S(1)}, f32[128,128]{1,0:T(8,128)S(1)}, f32[8,128]{1,0:T(8,128)S(1)}) custom-call(f32[136,8,256]{2,1,0:T(8,128)S(1)} %get-tuple-element.44.b, f32[136,256]{1,0:T(8,128)S(1)} %get-tuple-element.45.w, f32[4,128,256]{2,1,0:T(8,128)S(1)} %copy-done, ...), custom_call_target="tpu_custom_call" | custom-call | tf_op jit(solution)/shard_map/pallas_call | solution.py:521
  35.6 14.6 %all_to_all.21 = f32[128,1,128]{2,1,0:T(1,128)S(1)} all-to-all(f32[128,1,128]{2,1,0:T(1,128)S(1)} %bitcast.7), channel_id=1, replica_groups=mesh['region'=8,'tile'=16] {'region','tile'}, dimensions={0} | all-to-all | bytes 131072 | tf_op jit(solution)/shard_map/all_to_all | solution.py:624
  50.2 1.9 %shard_map.63 = (f32[128,8,256]{2,1,0:T(8,128)}, f32[128,8,256]{2,1,0:T(8,128)}) custom-call(f32[128,128]{1,0:T(8,128)S(1)} %bitcast.6, f32[8,128]{1,0:T(8,128)S(1)} %get-tuple-element.49.own, f32[136,8,256]{2,1,0:T(8,128)S(1)} %get-tuple-element.44.b, f32[128,8,256]{2,1,0:T(8,128)S(1)} %get-tuple-element.50.q, f32[128,8,256]{2,1,0:T(8,128)S(1)} %get-tuple-element.51.t), custom_call_target="tpu_custom_call" | custom-call | tf_op jit(solution)/shard_map/pallas_call | solution.py:521
  (1 shorter events, 0.0 us)
Async XLA Ops:
  22.8 5.7 %collective-permute-start = (f32[72,128]{1,0:T(8,128)S(1)}, f32[72,128]{1,0:T(8,128)S(1)}, u32[]{:S(2)}, u32[]{:S(2)}) collective-permute-start(f32[72,128]{1,0:T(8,128)S(1)} %get-tuple-element.46), channel_id=1, source_target_pairs={{0,16},{16,32},{32,48},{48,64},{64,80},{80,96},{96,112},{112,0},{1... | collective-permute-start | bytes 110600 | tf_op jit(solution)/shard_map/ppermute | solution.py:536
  25.9 3.4 %collective-permute-start.1 = (f32[72,128]{1,0:T(8,128)S(1)}, f32[72,128]{1,0:T(8,128)S(1)}, u32[]{:S(2)}, u32[]{:S(2)}) collective-permute-start(f32[72,128]{1,0:T(8,128)S(1)} %get-tuple-element.47), channel_id=1, source_target_pairs={{0,112},{16,0},{32,16},{48,32},{64,48},{80,64},{96,80},{112,96},{1... | collective-permute-start | bytes 110600 | tf_op jit(solution)/shard_map/ppermute | solution.py:536
  25.9 3.4 %copy-start = (f32[4,128,256]{2,1,0:T(8,128)S(1)}, f32[4,128,256]{2,1,0:T(8,128)}, u32[]{:S(2)}) copy-start(f32[4,128,256]{2,1,0:T(8,128)} %coef.1) | copy-start | bytes 1572868

commit v6 on v5

--- a/solution.py
+++ b/solution.py
@@ -22,7 +22,7 @@
 SHARE = 96
 DENSE = TILES * SHARE
 GROUPS = 5
-PART = 16
+PART = 32
 PIECE = EXT // 4
 F32, BF16, I32 = jnp.float32, jnp.bfloat16, jnp.int32
 VMEM_LIMIT = 48 * 1024 * 1024

time: 52.5 us -> 52.5 us (level)
  no operation moved by 1% of the time
where the time goes in v6:
time: 52.5 us; the launch traced here: 52.2 us
  blocking collectives  31.5 us (60%)
  Pallas kernels  14.7 us (28%)
  starting transfers between devices  3.06 us (6%)
  between operations  2.13 us (4%)
  waiting for transfers between devices  0.77 us (1%)
    all_to_all x1, blocking collectives, local(): recv = lax.all_to_all(packed, 'tile', 0, 0)  16.9 us
    pallas_call x5, Pallas kernels, call(): pl.pallas_call(body, out_shape=[jax.ShapeDtypeStruct(s, t) for s, t in zi...  14.7 us
    all_to_all x1, blocking collectives, local(): shared = lax.all_to_all(moments, ('region', 'tile'), 0, 0, tiled=True)  14.6 us
    ppermute x2, starting transfers between devices, ring(): return lax.ppermute(x, axis, [(i, (i + step) % size) for i in range(size)])  3.06 us
  transfers between devices with their start and end apart: 2, of which 1 were waited for; matrix products, arithmetic and copies ran while one was open for 0% of the time, Pallas kernels for 5%

profile of v6, /device:TPU:1, one launch (start us, length us, event | category | flops | bytes accessed | tf_op | source)
XLA Modules:
  0.0 52.2 jit_solution(8751242382034067582)
XLA Ops:
  1.3 3.2 %shard_map.59 = (f32[16,40,128]{2,1,0:T(8,128)}, f32[104,128]{1,0:T(8,128)S(1)}, f32[16,72,128]{2,1,0:T(8,128)}) custom-call(s32[1]{0:T(128)S(6)} %copy.15.count, s32[1,1024]{1,0:T(1,128)} %bitcast.8, f32[8,1024]{1,0:T(8,128)} %value_hbm.1, f32[4,128,256]{2,1,0:T(8,128)} %coef.1), custom_call_target="tpu_custom_call" | custom-call | tf_op jit(solution)/shard_map/pallas_call | solution.py:521
  4.5 16.9 %all_to_all.20.recv = f32[16,40,128]{2,1,0:T(8,128)S(1)} all-to-all(f32[16,40,128]{2,1,0:T(8,128)} %get-tuple-element.37), channel_id=1, replica_groups=mesh['region'=8,'tile'=16] {'tile'}, dimensions={0} | all-to-all | bytes 655360 | tf_op jit(solution)/shard_map/all_to_all | solution.py:555
  21.4 0.8 %shard_map.60 = (f32[72,128]{1,0:T(8,128)S(1)}, f32[72,128]{1,0:T(8,128)S(1)}, s32[1]{0:T(128)}) custom-call(f32[16,40,128]{2,1,0:T(8,128)S(1)} %all_to_all.20.recv, f32[104,128]{1,0:T(8,128)S(1)} %get-tuple-element.38.listed), custom_call_target="tpu_custom_call" | custom-call | tf_op jit(solution)/shard_map/pallas_call | solution.py:521
  22.8 3.1 %collective-permute-start = (f32[72,128]{1,0:T(8,128)S(1)}, f32[72,128]{1,0:T(8,128)S(1)}, u32[]{:S(2)}, u32[]{:S(2)}) collective-permute-start(f32[72,128]{1,0:T(8,128)S(1)} %get-tuple-element.46), channel_id=1, source_target_pairs={{0,16},{16,32},{32,48},{48,64},{64,80},{80,96},{96,112},{112,0},{1... | collective-permute-start | bytes 110600 | tf_op jit(solution)/shard_map/ppermute | solution.py:536
  25.9 0.0 collective-permute-start.1
  25.9 0.0 copy-start
  25.9 2.6 %shard_map.61 = (f32[136,8,256]{2,1,0:T(8,128)S(1)}, f32[136,256]{1,0:T(8,128)S(1)}) custom-call(f32[16,40,128]{2,1,0:T(8,128)S(1)} %all_to_all.20.recv, f32[16,72,128]{2,1,0:T(8,128)} %get-tuple-element.43.lists), custom_call_target="tpu_custom_call" | custom-call | flops 1862270976 | bytes 8388608 | tf_op jit(solution)/shard_map/pallas_call | solution.py:521
  28.5 0.0 collective-permute-done.got_l
  28.5 0.8 %collective-permute-done.1.got_r = f32[72,128]{1,0:T(8,128)S(1)} collective-permute-done((f32[72,128]{1,0:T(8,128)S(1)}, f32[72,128]{1,0:T(8,128)S(1)}, u32[]{:S(2)}, u32[]{:S(2)}) %collective-permute-start.1) | collective-permute-done | bytes 36896 | tf_op jit(solution)/shard_map/ppermute | solution.py:536
  29.3 0.0 copy-done
  29.3 6.3 %shard_map.62 = (f32[128,8,256]{2,1,0:T(8,128)S(1)}, f32[128,8,256]{2,1,0:T(8,128)S(1)}, f32[128,128]{1,0:T(8,128)S(1)}, f32[8,128]{1,0:T(8,128)S(1)}) custom-call(f32[136,8,256]{2,1,0:T(8,128)S(1)} %get-tuple-element.44.b, f32[136,256]{1,0:T(8,128)S(1)} %get-tuple-element.45.w, f32[4,128,256]{2,1,0:T(8,128)S(1)} %copy-done, ...), custom_call_target="tpu_custom_call" | custom-call | tf_op jit(solution)/shard_map/pallas_call | solution.py:521
  35.6 14.6 %all_to_all.21 = f32[128,1,128]{2,1,0:T(1,128)S(1)} all-to-all(f32[128,1,128]{2,1,0:T(1,128)S(1)} %bitcast.7), channel_id=1, replica_groups=mesh['region'=8,'tile'=16] {'region','tile'}, dimensions={0} | all-to-all | bytes 131072 | tf_op jit(solution)/shard_map/all_to_all | solution.py:624
  50.2 1.8 %shard_map.63 = (f32[128,8,256]{2,1,0:T(8,128)}, f32[128,8,256]{2,1,0:T(8,128)}) custom-call(f32[128,128]{1,0:T(8,128)S(1)} %bitcast.6, f32[8,128]{1,0:T(8,128)S(1)} %get-tuple-element.49.own, f32[136,8,256]{2,1,0:T(8,128)S(1)} %get-tuple-element.44.b, f32[128,8,256]{2,1,0:T(8,128)S(1)} %get-tuple-element.50.q, f32[128,8,256]{2,1,0:T(8,128)S(1)} %get-tuple-element.51.t), custom_call_target="tpu_custom_call" | custom-call | tf_op jit(solution)/shard_map/pallas_call | solution.py:521
  (1 shorter events, 0.0 us)
Async XLA Ops:
  22.8 5.7 %collective-permute-start = (f32[72,128]{1,0:T(8,128)S(1)}, f32[72,128]{1,0:T(8,128)S(1)}, u32[]{:S(2)}, u32[]{:S(2)}) collective-permute-start(f32[72,128]{1,0:T(8,128)S(1)} %get-tuple-element.46), channel_id=1, source_target_pairs={{0,16},{16,32},{32,48},{48,64},{64,80},{80,96},{96,112},{112,0},{1... | collective-permute-start | bytes 110600 | tf_op jit(solution)/shard_map/ppermute | solution.py:536
  25.9 3.4 %collective-permute-start.1 = (f32[72,128]{1,0:T(8,128)S(1)}, f32[72,128]{1,0:T(8,128)S(1)}, u32[]{:S(2)}, u32[]{:S(2)}) collective-permute-start(f32[72,128]{1,0:T(8,128)S(1)} %get-tuple-element.47), channel_id=1, source_target_pairs={{0,112},{16,0},{32,16},{48,32},{64,48},{80,64},{96,80},{112,96},{1... | collective-permute-start | bytes 110600 | tf_op jit(solution)/shard_map/ppermute | solution.py:536
  25.9 3.4 %copy-start = (f32[4,128,256]{2,1,0:T(8,128)S(1)}, f32[4,128,256]{2,1,0:T(8,128)}, u32[]{:S(2)}) copy-start(f32[4,128,256]{2,1,0:T(8,128)} %coef.1) | copy-start | bytes 1572868
